TPU v7x, 32 devices: a whole 2x2x4 slice. The times are simulated.
32 devices in a mesh: freq: 4 (over z), row: 2 (over x), col: 4 (over y, core).
Axes of the slice: x: 2, y: 2, z: 4, core: 2. Of those that a mesh axis runs over, the one named last changes fastest.
Arguments:
- samples: int32 [2, 2048, 68608], P(None, ('row', 'col', 'freq')), may hold values from -7 to 7
- input_gains: float32 [2048], P(('row', 'col', 'freq')), may hold values from 0.3 to 3
- filter_taps: float32 [4, 1024], replicated, may hold values from 0.25 to 1
Outputs:
- vis_real: bfloat16 [16, 2048, 2048], P('freq', 'row', 'col')
- vis_imag: bfloat16 [16, 2048, 2048], P('freq', 'row', 'col')
All inputs are finite; a program needn't handle non-finite values.
Results may differ from a plain program's by a relative error of at most 0.0065.
Values may be sent and summed in bfloat16 or wider, within the bound.
No kernel may reach another device: no remote copies, remote signals or barrier semaphores. Data moves between devices by JAX's collectives and lax.ppermute only.
A program may use at most 192 MiB of HBM per device.

v0:
```python
import math

import jax
import jax.numpy as jnp
from jax import lax
from jax.sharding import PartitionSpec as P

NFFT = 1024
TAPS = 4
SPEC = 64
CH_DEV = 4


def dft_table(channels):
    position = jnp.arange(NFFT, dtype=jnp.int32)
    channel = jnp.arange(channels, dtype=jnp.int32)
    phases = (position[:, None] * channel[None, :] % NFFT).astype(jnp.float32) * (
        2.0 * math.pi / NFFT
    )
    scaling = 0.5 / math.sqrt(NFFT)
    cosine = jnp.cos(phases) * scaling
    sine = jnp.sin(phases) * scaling
    real_rows = jnp.stack([cosine, -sine], axis=1)
    imag_rows = jnp.stack([sine, cosine], axis=1)
    return jnp.stack([real_rows, imag_rows], axis=0).astype(jnp.bfloat16)


def local(samples, input_gains, filter_taps):
    channels = CH_DEV * lax.axis_size("freq")
    inputs_here = samples.shape[1]
    voltage = samples.astype(jnp.float32) * 0.25 * input_gains[None, :, None]
    frames = voltage.reshape(2, inputs_here, SPEC + TAPS - 1, NFFT)
    filtered = frames[:, :, 0:SPEC, :] * filter_taps[0]
    for tap_index in range(1, TAPS):
        filtered = filtered + frames[:, :, tap_index : tap_index + SPEC, :] * filter_taps[tap_index]
    filtered = filtered.astype(jnp.bfloat16)
    spectra = jnp.einsum(
        "pimn,pnqk->kiqm", filtered, dft_table(channels), preferred_element_type=jnp.float32
    )
    spectra = spectra.reshape(channels, inputs_here, 2 * SPEC).astype(jnp.bfloat16)
    grouped = lax.all_to_all(spectra, "freq", split_axis=0, concat_axis=1, tiled=True)
    row_count = lax.axis_size("row")
    column_count = lax.axis_size("col")
    everything = lax.all_gather(grouped, ("row", "col"), axis=1, tiled=True)
    row_size = everything.shape[1] // row_count
    column_size = everything.shape[1] // column_count
    row_data = lax.dynamic_slice_in_dim(everything, lax.axis_index("row") * row_size, row_size, 1)
    column_data = lax.dynamic_slice_in_dim(
        everything, lax.axis_index("col") * column_size, column_size, 1
    )
    rotated = jnp.concatenate([-column_data[:, :, SPEC:], column_data[:, :, :SPEC]], axis=2)
    stacked = jnp.concatenate([column_data, rotated], axis=1)
    product = jnp.einsum("kim,kjm->kij", row_data, stacked, preferred_element_type=jnp.float32) * (
        1.0 / SPEC
    )
    width = column_data.shape[1]
    vis_real = product[:, :, :width].astype(jnp.bfloat16)
    vis_imag = product[:, :, width:].astype(jnp.bfloat16)
    return (vis_real, vis_imag)


def solution(mesh):
    placed = (P(None, ("row", "col", "freq"), None), P(("row", "col", "freq")), P())
    return jax.shard_map(
        local,
        mesh=mesh,
        in_specs=placed,
        out_specs=(P("freq", "row", "col"), P("freq", "row", "col")),
        check_vma=False,
    )
```

profile of v0, /device:TPU:11, one launch (start us, length us, event | category | flops | bytes accessed | tf_op | source)
XLA Modules:
  0.0 167.8 jit_solution(1385774788383767200)
XLA Ops:
  7.2 0.0 all-gather.2.cloned.1.call-start
  7.2 0.3 negate_convert_fusion
  7.5 0.3 fusion.30
  7.8 0.7 broadcast_multiply_fusion
  8.4 23.4 %convert_multiply_fusion = f32[2,64,68608]{2,1,0:T(8,128)} fusion(s32[2,64,68608]{2,1,0:T(8,128)} %param.3, f32[64]{0:T(128)S(1)} %broadcast_multiply_fusion), kind=kLoop, calls=%fused_computation | loop fusion | flops 17563648 | bytes 70254848 | tf_op jit(solution)/shard_map/mul | solution.py:31
  31.9 0.0 copy-start
  31.9 30.5 %reshape.95 = f32[2,64,67,1024]{3,2,1,0:T(8,128)} reshape(f32[2,64,68608]{2,1,0:T(8,128)} %convert_multiply_fusion) | data formatting | bytes 70254592 | tf_op jit(solution)/shard_map/reshape | solution.py:32
  62.3 0.0 copy-done
  62.3 46.0 %fusion.13 = bf16[16,64,2,64]{3,0,1,2:T(8,128)(2,1)S(1)} fusion(bf16[1,1024,2,16]{1,3,0,2:T(8,128)(2,1)S(1)} %get-tuple-element.7, bf16[1,1024,2,16]{1,3,0,2:T(8,128)(2,1)S(1)} %get-tuple-element.6, f32[2,64,67,1024]{3,2,1,0:T(8,128)} %reshape.95, f32[1024]{0:T(1024)S(1)} %bitcast.51, f32[1024]{0:T(1024)S(1)} %bitcast.52, f32[1024]{0:T(1024)S(1)} %bitcast.50, ...), kind=kOutput, calls=%fused_computation.15 | convolution fusion | flops 604372992 | bytes 134627328 | tf_op jit(solution)/shard_map/pimn,pnqk->kiqm/dot_general | solution.py:37
  108.4 0.5 copy.12
  108.9 0.2 convert_element_type.47
  109.2 10.5 %all_to_all.18 = bf16[16,64,128]{2,1,0:T(8,128)(2,1)S(1)} all-to-all(bf16[16,64,128]{2,1,0:T(8,128)(2,1)S(1)} %convert_element_type.47), channel_id=1, replica_groups=mesh['freq'=4,'row'=2,'col'=4] {'freq'}, dimensions={0} | all-to-all | bytes 524288 | tf_op jit(solution)/shard_map/all_to_all | solution.py:41
  119.7 0.7 copy.13
  120.4 0.0 all-gather.2.cloned.1.call-update
  120.5 30.5 %all-gather.2.cloned.1.call-done = bf16[4,2048,128]{2,1,0:T(8,128)(2,1)} async-done(((bf16[4,256,128]{2,1,0:T(8,128)(2,1)}), bf16[4,2048,128]{2,1,0:T(8,128)(2,1)}) %all-gather.2.cloned.1.call-update) | async-done | bytes 2097168 | tf_op jit(solution)/shard_map/all_gather | solution.py:44
  151.0 1.1 constant_dynamic-slice_fusion.1
  152.0 1.5 dynamic-slice_negate_fusion
  153.5 3.6 %multiply_convert_fusion = bf16[4,1024,1024]{2,1,0:T(8,128)(2,1)S(1)} fusion(bf16[4,512,64]{2,1,0:T(8,128)(2,1)S(1)} %get-tuple-element.5, bf16[4,512,64]{2,1,0:T(8,128)(2,1)S(1)} %get-tuple-element.4, bf16[4,512,128]{2,1,0:T(8,128)(2,1)S(1)} %constant_dynamic-slice_fusion.1, bf16[4,2048,128]{2,1,0:T(8,128)(2,1)} %all-gather.2.cloned.1.call-done, ...), kind=kOutput, calls=%fused_computation.12 | convolution fusion | flops 1085276160 | bytes 10485764 | tf_op jit(solution)/shard_map/kim,kjm->kij/dot_general | solution.py:53
  157.1 3.9 %fusion.34 = (bf16[4,1024,512]{2,1,0:T(8,128)(2,1)}, bf16[4,1024,512]{2,1,0:T(8,128)(2,1)}) fusion(bf16[4,1024,1024]{2,1,0:T(8,128)(2,1)S(1)} %multiply_convert_fusion), kind=kLoop, calls=%fused_computation.47 | loop fusion | bytes 16777216 | tf_op jit(solution)/shard_map/slice | solution.py:58
  (2 shorter events, 0.0 us)
Async XLA Ops:
  7.2 143.8 %all-gather.2.cloned.1.call-start = ((), (), s32[]{:S(2)}) async-start(), calls=%async_computation.1 | async-start | bytes 2359296 | tf_op jit(solution)/shard_map/all_gather | solution.py:44
  31.9 30.5 %copy-start = (f32[4,1024]{1,0:T(4,128)S(1)}, f32[4,1024]{1,0:T(4,128)}, u32[]{:S(2)}) copy-start(f32[4,1024]{1,0:T(4,128)} %param.5) | copy-start | bytes 49156
Sparse Core Ops, SparseCore 0:
  120.6 30.3 all-gather.1
where the time goes:
time: 170 us; the launch traced here: 168 us
  matrix products  49.6 us (29%)
  local copies, waits for them, and re-layouts  36.9 us (22%)
  waiting for transfers between devices  30.5 us (18%)
  other arithmetic  26.1 us (15%)
  between operations  14.1 us (8%)
  blocking collectives  10.5 us (6%)
    dot_general x1, matrix products, local(): jnp.einsum('pimn,pnqk->kiqm', filtered, dft_table(channels), preferred_el...  46 us
    all_gather x1, waiting for transfers between devices, local(): everything = lax.all_gather(grouped, ('row', 'col'), axis=1, tiled=True)  30.5 us
    reshape x1, local copies, waits for them, and re-layouts, local(): frames = voltage.reshape(2, inputs_here, SPEC + TAPS - 1, NFFT)  30.5 us
    mul x2, other arithmetic, local(): voltage = samples.astype(jnp.float32) * 0.25 * input_gains[None, :, None]  24.1 us
    all_to_all x1, blocking collectives, local(): lax.all_to_all(spectra, 'freq', split_axis=0, concat_axis=1, tiled=True)  10.5 us
    slice x1, local copies, waits for them, and re-layouts, local(): vis_imag = product[:, :, width:].astype(jnp.bfloat16)  3.86 us
    dot_general x1, matrix products, local(): jnp.einsum('kim,kjm->kij', row_data, stacked, preferred_element_type=jnp....  3.59 us
  transfers between devices with their start and end apart: 1, of which 1 were waited for; matrix products, arithmetic and copies ran while one was open for 0% of the time, Pallas kernels for 0%

commit v1 on v0

--- a/solution.py
+++ b/solution.py
@@ -1,14 +1,288 @@
+import functools
 import math
 
 import jax
 import jax.numpy as jnp
+import numpy as np
 from jax import lax
+from jax.experimental import pallas as pl
+from jax.experimental.pallas import tpu as pltpu
 from jax.sharding import PartitionSpec as P
 
 NFFT = 1024
 TAPS = 4
 SPEC = 64
 CH_DEV = 4
+LANES = 128
+VMEM_BYTES = 60 * 2**20
+
+
+def dft_rows(channels):
+    phases = (np.arange(channels)[:, None] * np.arange(NFFT)[None, :] % NFFT) * (
+        2.0 * math.pi / NFFT
+    )
+    scaling = 0.5 / math.sqrt(NFFT)
+    cosine = np.cos(phases) * scaling
+    sine = np.sin(phases) * scaling
+    real_rows = np.concatenate([cosine, sine], axis=1)
+    imag_rows = np.concatenate([-sine, cosine], axis=1)
+    rows = np.stack([real_rows, imag_rows], axis=1).reshape(2 * channels, 2 * NFFT)
+    return jnp.asarray(rows.astype(np.float32)).astype(jnp.bfloat16)
+
+
+def channelize_body(
+    gain_ref, taps_ref, table_ref, samples_ref, *rest, first, half, blocks, groups
+):
+    outs, (weights, raw, lhs, sums, held, sems) = rest[:groups], rest[groups:]
+    inputs = samples_ref.shape[1]
+    rows = table_ref.shape[0]
+    pieces = []
+    for index, (start, stop) in enumerate(blocks):
+        pieces.append((index, 0, start, min(stop, half)))
+        pieces.append((index, 1, half + start, half + stop))
+    copies = {}
+    for index, side, begin, end in pieces:
+        if begin < end:
+            span = pl.ds(begin * NFFT, (end - begin) * NFFT)
+            source = pl.ds((first + begin) * NFFT, (end - begin) * NFFT)
+            copies[index, side] = pltpu.make_async_copy(
+                samples_ref.at[:, :, source], raw.at[:, :, span], sems.at[index, side]
+            )
+            copies[index, side].start()
+    for p in range(2):
+        for b in range(NFFT // LANES):
+            table = table_ref[:, p * NFFT + b * LANES : p * NFFT + (b + 1) * LANES].astype(
+                jnp.float32
+            )
+            for t in range(TAPS):
+                exact = table * taps_ref[t : t + 1, b * LANES : (b + 1) * LANES]
+                high = exact.astype(jnp.bfloat16)
+                low = (exact - high.astype(jnp.float32)).astype(jnp.bfloat16)
+                at = pl.ds(p * NFFT + b * LANES, LANES)
+                weights[t * rows : (t + 1) * rows, at] = high
+                weights[(TAPS + t) * rows : (TAPS + t + 1) * rows, at] = low
+    for index, (start, stop) in enumerate(blocks):
+        for side in range(2):
+            if (index, side) in copies:
+                copies[index, side].wait()
+        buffer = lhs[index % 2]
+        for slot in range(start, stop):
+            for side in range(2):
+                frame = side * half + slot
+                to = (slot - start) * 2 * inputs + side * inputs
+                for p in range(2):
+                    buffer[to : to + inputs, p * NFFT : (p + 1) * NFFT] = (
+                        raw[p, :, frame * NFFT : (frame + 1) * NFFT]
+                        .astype(jnp.float32)
+                        .astype(jnp.bfloat16)
+                    )
+        size = (stop - start) * 2 * inputs
+        both = lax.dot_general(
+            weights[...],
+            buffer[0:size, :],
+            (((1,), (1,)), ((), ())),
+            preferred_element_type=jnp.float32,
+        )
+        sums[:, start * LANES : stop * LANES] = both[: TAPS * rows] + both[TAPS * rows :]
+    gain = gain_ref[...]
+    gain = jnp.concatenate([gain, gain], axis=1) * (0.25 / math.sqrt(SPEC))
+    for slot in range(half):
+        total = sums[0:rows, slot * LANES : (slot + 1) * LANES]
+        for t in range(1, TAPS):
+            total = total + sums[
+                t * rows : (t + 1) * rows, (slot + t) * LANES : (slot + t + 1) * LANES
+            ]
+        held[pl.ds(slot, rows, stride=half), :] = total * gain
+    me = lax.axis_index("freq")
+    depth = 2 * half
+    for s in range(groups):
+        to = lax.rem(me + s, groups) * (CH_DEV * depth)
+        for k in range(CH_DEV):
+            outs[s][k] = held[
+                pl.ds(pl.multiple_of(to + k * depth, 8), depth), :
+            ].astype(jnp.bfloat16)
+
+
+def channelize(samples, gains, taps, first, half, cuts, groups):
+    inputs = samples.shape[1]
+    channels = CH_DEV * groups
+    rows = 2 * channels
+    slots = half + TAPS - 1
+    blocks = list(zip(cuts[:-1], cuts[1:]))
+    widest = max(stop - start for start, stop in blocks)
+    frames = 2 * half + TAPS - 1
+    return pl.pallas_call(
+        functools.partial(
+            channelize_body, first=first, half=half, blocks=blocks, groups=groups
+        ),
+        grid=(1,),
+        in_specs=[
+            pl.BlockSpec((1, inputs), lambda i: (0, 0)),
+            pl.BlockSpec((TAPS, NFFT), lambda i: (0, 0)),
+            pl.BlockSpec((rows, 2 * NFFT), lambda i: (0, 0)),
+            pl.BlockSpec(memory_space=pl.ANY),
+        ],
+        out_specs=[pl.BlockSpec((CH_DEV, 2 * half, LANES), lambda i: (0, 0, 0))] * groups,
+        out_shape=[jax.ShapeDtypeStruct((CH_DEV, 2 * half, LANES), jnp.bfloat16)] * groups,
+        scratch_shapes=[
+            pltpu.VMEM((2 * TAPS * rows, 2 * NFFT), jnp.bfloat16),
+            pltpu.VMEM((2, inputs, frames * NFFT), jnp.int32),
+            [pltpu.VMEM((widest * 2 * inputs, 2 * NFFT), jnp.bfloat16)] * 2,
+            pltpu.VMEM((TAPS * rows, slots * LANES), jnp.float32),
+            pltpu.VMEM((rows * half, LANES), jnp.float32),
+            pltpu.SemaphoreType.DMA((len(blocks), 2)),
+        ],
+        compiler_params=pltpu.CompilerParams(vmem_limit_bytes=VMEM_BYTES),
+        cost_estimate=pl.CostEstimate(
+            flops=2 * 2 * NFFT * 256 * frames * inputs,
+            bytes_accessed=8 * inputs * frames * NFFT,
+            transcendentals=0,
+        ),
+        name="channelize",
+    )(gains.reshape(1, inputs), taps, dft_rows(channels), samples)
+
+
+def regroup_body(*refs, half):
+    groups = len(refs) - 2
+    sources, out, ordered = refs[:groups], refs[groups], refs[groups + 1]
+    me = lax.axis_index("freq")
+    for s in range(groups):
+        ordered[lax.rem(me - s + groups, groups)] = sources[s][...]
+    depth = 2 * half
+    lane = lax.broadcasted_iota(jnp.int32, (depth, LANES), 1)
+    for pair in range(groups // 2):
+        for k in range(CH_DEV):
+            left = ordered[2 * pair, k].astype(jnp.float32)
+            right = ordered[2 * pair + 1, k].astype(jnp.float32)
+            early = jnp.where(lane < LANES // 2, left, pltpu.roll(right, LANES // 2, 1))
+            late = jnp.where(lane < LANES // 2, pltpu.roll(left, LANES // 2, 1), right)
+            at = pl.ds(pair * LANES, LANES)
+            out[k, 0:depth, at] = early.astype(jnp.bfloat16)
+            out[k, depth : 2 * depth, at] = late.astype(jnp.bfloat16)
+
+
+def regroup(sources, half):
+    groups = len(sources)
+    shape = (CH_DEV, 4 * half, groups * LANES // 2)
+    return pl.pallas_call(
+        functools.partial(regroup_body, half=half),
+        out_shape=jax.ShapeDtypeStruct(shape, jnp.bfloat16),
+        scratch_shapes=[pltpu.VMEM((groups,) + sources[0].shape, jnp.bfloat16)],
+        name="regroup",
+    )(*sources)
+
+
+def products_body(*refs, half, parts):
+    rows_in = [refs[4 * part : 4 * part + 4] for part in range(parts)]
+    cols_in = [refs[4 * parts + 2 * part : 4 * parts + 2 * part + 2] for part in range(parts)]
+    real, imag, left, right = refs[6 * parts :]
+    row, col = lax.axis_index("row"), lax.axis_index("col")
+    y, core = col // 2, lax.rem(col, 2)
+    width = rows_in[0][0].shape[2]
+    deep = 4 * half
+    for part in range(parts):
+        down = slice(part * deep, (part + 1) * deep)
+        for flip_y in range(2):
+            for flip_core in range(2):
+                block = (y + flip_y) % 2 * 2 + (core + flip_core) % 2
+                left[block, down, :] = rows_in[part][2 * flip_y + flip_core][0]
+    for t in range(2):
+        across = slice(t * width, (t + 1) * width)
+
+        @pl.when(row == y)
+        def _():
+            right[:, across] = left[core * 2 + t]
+
+        @pl.when(row != y)
+        def _():
+            for part in range(parts):
+                down = slice(part * deep, (part + 1) * deep)
+                right[down, across] = cols_in[part][t][0]
+
+    columns = 2 * width
+    for at in range(0, parts * deep, 2 * half):
+        re, im = right[at : at + half, 0:columns], right[at + half : at + 2 * half, 0:columns]
+        right[at : at + half, columns : 2 * columns] = -im
+        right[at + half : at + 2 * half, columns : 2 * columns] = re
+    for block in range(4):
+        product = lax.dot_general(
+            left[block],
+            right[...],
+            (((0,), (0,)), ((), ())),
+            preferred_element_type=jnp.float32,
+        )
+        at = slice(block * width, (block + 1) * width)
+        real[0, at, :] = product[:, 0:columns].astype(jnp.bfloat16)
+        imag[0, at, :] = product[:, columns : 2 * columns].astype(jnp.bfloat16)
+
+
+def products(row_blocks, col_blocks, half):
+    parts = len(row_blocks)
+    _, deep, width = row_blocks[0][0].shape
+    flat = [a for part in row_blocks for a in part] + [a for part in col_blocks for a in part]
+    out = jax.ShapeDtypeStruct((CH_DEV, 4 * width, 2 * width), jnp.bfloat16)
+    return pl.pallas_call(
+        functools.partial(products_body, half=half, parts=parts),
+        grid=(CH_DEV,),
+        in_specs=[pl.BlockSpec((1, deep, width), lambda k: (k, 0, 0))] * len(flat),
+        out_specs=[pl.BlockSpec((1, 4 * width, 2 * width), lambda k: (k, 0, 0))] * 2,
+        out_shape=[out, out],
+        scratch_shapes=[
+            pltpu.VMEM((4, parts * deep, width), jnp.bfloat16),
+            pltpu.VMEM((parts * deep, 4 * width), jnp.bfloat16),
+        ],
+        compiler_params=pltpu.CompilerParams(vmem_limit_bytes=VMEM_BYTES),
+        cost_estimate=pl.CostEstimate(
+            flops=2 * CH_DEV * parts * deep * 16 * width * width,
+            bytes_accessed=2 * 2 * CH_DEV * 8 * width * width,
+            transcendentals=0,
+        ),
+        name="products",
+    )(*flat)
+
+
+def exchange(sent, groups):
+    ring = lambda s: [(i, (i + s) % groups) for i in range(groups)]
+    turned = [sent[0]] + [lax.ppermute(sent[s], "freq", ring(s)) for s in range(1, groups)]
+    return turned
+
+
+def gather(mine):
+    other_core = [(0, 1), (1, 0), (2, 3), (3, 2)]
+    other_y = [(0, 2), (2, 0), (1, 3), (3, 1)]
+    place = lambda x, y, c: x * 4 + y * 2 + c
+    far_y = lax.ppermute(mine, "col", other_y)
+    columns = [
+        lax.ppermute(
+            mine,
+            ("row", "col"),
+            [(place(x, y, c), place(1 - x, x, y)) for x in range(2) for y in range(2)],
+        )
+        for c in range(2)
+    ]
+    near = lax.ppermute(mine, "col", other_core)
+    far = lax.ppermute(far_y, "col", other_core)
+    return [mine, near, far_y, far], columns
+
+
+def fast(samples, input_gains, filter_taps):
+    groups = lax.axis_size("freq")
+    parts = PARTS
+    half = SPEC // 2 // parts
+    row_blocks, col_blocks = [], []
+    for part in range(parts):
+        sent = channelize(
+            samples, input_gains, filter_taps, part * 2 * half, half, CUTS, groups
+        )
+        mine = regroup(exchange(sent, groups), half)
+        rows, columns = gather(mine)
+        row_blocks.append(rows)
+        col_blocks.append(columns)
+    return tuple(products(row_blocks, col_blocks, half))
+
+
+PARTS = 1
+CUTS = (0, 4, 8, 12, 16, 20, 24, 28, 32, 35)
 
 
 def dft_table(channels):
@@ -25,7 +299,7 @@
     return jnp.stack([real_rows, imag_rows], axis=0).astype(jnp.bfloat16)
 
 
-def local(samples, input_gains, filter_taps):
+def plain(samples, input_gains, filter_taps):
     channels = CH_DEV * lax.axis_size("freq")
     inputs_here = samples.shape[1]
     voltage = samples.astype(jnp.float32) * 0.25 * input_gains[None, :, None]
@@ -61,8 +335,9 @@
 
 def solution(mesh):
     placed = (P(None, ("row", "col", "freq"), None), P(("row", "col", "freq")), P())
+    fits = dict(mesh.shape) == {"freq": 4, "row": 2, "col": 4}
     return jax.shard_map(
-        local,
+        fast if fits else plain,
         mesh=mesh,
         in_specs=placed,
         out_specs=(P("freq", "row", "col"), P("freq", "row", "col")),

time: 170 us -> 49.7 us (0.29); the launches traced: 168 us -> 49.3 us
  matrix products: 49.6 us -> 0 us
  local copies, waits for them, and re-layouts: 36.9 us -> 1.35 us
  other arithmetic: 26.1 us -> 0 us
  Pallas kernels: 0 us -> 22.6 us
  waiting for transfers between devices: 30.5 us -> 10.2 us
  starting transfers between devices: 0.04 us -> 14.4 us
  between operations: 14.1 us -> 0.7 us
  blocking collectives: 10.5 us -> 0 us
    dot_general x2 -> x0, matrix products: 49.6 us -> none  [the longest x1 46 us: local(): jnp.einsum('pimn,pnqk->kiqm', filtered, dft_table(channels), preferred_el...]
    all_gather x1 -> x0, waiting for transfers between devices: 30.5 us -> none  [local(): everything = lax.all_gather(grouped, ('row', 'col'), axis=1, tiled=True)]
    reshape x1 -> x0, local copies, waits for them, and re-layouts: 30.5 us -> none  [local(): frames = voltage.reshape(2, inputs_here, SPEC + TAPS - 1, NFFT)]
    mul x2 -> x0, other arithmetic: 24.1 us -> none  [local(): voltage = samples.astype(jnp.float32) * 0.25 * input_gains[None, :, None]]
    pallas_call x0 -> x3, Pallas kernels: none -> 22.6 us  [the longest x1 14.4 us: channelize(): pl.pallas_call(functools.partial(channelize_body, first=first, half=half,...]
    ppermute x0 -> x8, starting transfers between devices: none -> 14.4 us  [the longest x1 4.53 us: gather(): far = lax.ppermute(far_y, 'col', other_core)]
    all_to_all x1 -> x0, blocking collectives: 10.5 us -> none  [local(): lax.all_to_all(spectra, 'freq', split_axis=0, concat_axis=1, tiled=True)]
    ppermute x0 -> x8, waiting for transfers between devices: none -> 10.2 us  [the longest x3 5.18 us: exchange(): lax.ppermute(sent[s], 'freq', ring(s))]
  transfers between devices with their start and end apart: 1 -> 8, of which waited for: 1 -> 4; matrix products, arithmetic and copies ran while one was open for 0% -> 0% of each run, Pallas kernels for 0% -> 0%
where the time goes in v1:
time: 49.7 us; the launch traced here: 49.3 us
  Pallas kernels  22.6 us (45%)
  starting transfers between devices  14.4 us (29%)
  waiting for transfers between devices  10.2 us (21%)
  local copies, waits for them, and re-layouts  1.35 us (3%)
  between operations  0.7 us (1%)
    pallas_call x1, Pallas kernels, channelize(): pl.pallas_call(functools.partial(channelize_body, first=first, half=half,...  14.4 us
    pallas_call x1, Pallas kernels, products(): pl.pallas_call(functools.partial(products_body, half=half, parts=parts),...  6.42 us
    ppermute x3, waiting for transfers between devices, exchange(): lax.ppermute(sent[s], 'freq', ring(s))  5.18 us
    ppermute x1, starting transfers between devices, gather(): far = lax.ppermute(far_y, 'col', other_core)  4.53 us
    ppermute x2, starting transfers between devices, gather(): lax.ppermute(mine, ('row', 'col'), [(place(x, y, c), place(1 - x, x, y))...  4.36 us
    ppermute x1, waiting for transfers between devices, gather(): far_y = lax.ppermute(mine, 'col', other_y)  3.93 us
    ppermute x3, starting transfers between devices, exchange(): lax.ppermute(sent[s], 'freq', ring(s))  3.82 us
    pallas_call x1, Pallas kernels, regroup(): pl.pallas_call(functools.partial(regroup_body, half=half), out_shape=jax....  1.8 us
  transfers between devices with their start and end apart: 8, of which 4 were waited for; matrix products, arithmetic and copies ran while one was open for 0% of the time, Pallas kernels for 0%

profile of v1, /device:TPU:11, one launch (start us, length us, event | category | flops | bytes accessed | tf_op | source)
XLA Modules:
  0.0 49.3 jit_solution(16695709147634724310)
XLA Ops:
  0.6 14.4 %channelize.1 = (bf16[4,64,128]{2,1,0:T(8,128)(2,1)}, bf16[4,64,128]{2,1,0:T(8,128)(2,1)}, bf16[4,64,128]{2,1,0:T(8,128)(2,1)}, bf16[4,64,128]{2,1,0:T(8,128)(2,1)}) custom-call(f32[1,64]{1,0:T(1,128)} %bitcast.1, f32[4,1024]{1,0:T(4,128)} %taps_ref.1, bf16[32,2048]{1,0:T(8,128)(2,1)} %constant.3.table_ref, s32[2,64,68608]{2,1,0:T(8,128)} %samples_ref.1), custom_call_target="tpu_custom_call" | custom-call | flops 4496293888 | bytes 35127296 | tf_op jit(solution)/shard_map/channelize/pallas_call | solution.py:114
  15.0 1.3 %collective-permute-start = (bf16[4,64,128]{2,1,0:T(8,128)(2,1)}, bf16[4,64,128]{2,1,0:T(8,128)(2,1)S(1)}, u32[]{:S(2)}, u32[]{:S(2)}) collective-permute-start(bf16[4,64,128]{2,1,0:T(8,128)(2,1)} %get-tuple-element.7), channel_id=1, source_target_pairs={{0,8},{8,16},{16,24},{24,0},{1,9},{9,17},{17,25},{25,1},{2,10},{10... | collective-permute-start | bytes 196616 | tf_op jit(solution)/shard_map/ppermute | solution.py:246
  16.3 1.1 %collective-permute-start.1 = (bf16[4,64,128]{2,1,0:T(8,128)(2,1)}, bf16[4,64,128]{2,1,0:T(8,128)(2,1)S(1)}, u32[]{:S(2)}, u32[]{:S(2)}) collective-permute-start(bf16[4,64,128]{2,1,0:T(8,128)(2,1)} %get-tuple-element.8), channel_id=1, source_target_pairs={{0,16},{8,24},{16,0},{24,8},{1,17},{9,25},{17,1},{25,9},{2,18},{10... | collective-permute-start | bytes 196616 | tf_op jit(solution)/shard_map/ppermute | solution.py:246
  17.4 1.4 %collective-permute-start.2 = (bf16[4,64,128]{2,1,0:T(8,128)(2,1)}, bf16[4,64,128]{2,1,0:T(8,128)(2,1)S(1)}, u32[]{:S(2)}, u32[]{:S(2)}) collective-permute-start(bf16[4,64,128]{2,1,0:T(8,128)(2,1)} %get-tuple-element.9), channel_id=1, source_target_pairs={{0,24},{8,0},{16,8},{24,16},{1,25},{9,1},{17,9},{25,17},{2,26},{10... | collective-permute-start | bytes 196616 | tf_op jit(solution)/shard_map/ppermute | solution.py:246
  18.8 0.0 collective-permute-done.refs_1_
  18.8 0.0 copy-start
  18.8 2.2 %collective-permute-done.1.refs_2_ = bf16[4,64,128]{2,1,0:T(8,128)(2,1)S(1)} collective-permute-done((bf16[4,64,128]{2,1,0:T(8,128)(2,1)}, bf16[4,64,128]{2,1,0:T(8,128)(2,1)S(1)}, u32[]{:S(2)}, u32[]{:S(2)}) %collective-permute-start.1) | collective-permute-done | bytes 65568 | tf_op jit(solution)/shard_map/ppermute | solution.py:246
  21.0 0.0 copy-start.1
  21.0 3.0 %collective-permute-done.2.refs_3_ = bf16[4,64,128]{2,1,0:T(8,128)(2,1)S(1)} collective-permute-done((bf16[4,64,128]{2,1,0:T(8,128)(2,1)}, bf16[4,64,128]{2,1,0:T(8,128)(2,1)S(1)}, u32[]{:S(2)}, u32[]{:S(2)}) %collective-permute-start.2) | collective-permute-done | bytes 65568 | tf_op jit(solution)/shard_map/ppermute | solution.py:246
  24.0 0.0 copy-start.2
  24.0 0.0 copy-done
  24.0 0.0 copy-done.1
  24.0 0.6 %copy-done.2 = bf16[4,64,128]{2,1,0:T(8,128)(2,1)} copy-done((bf16[4,64,128]{2,1,0:T(8,128)(2,1)}, bf16[4,64,128]{2,1,0:T(8,128)(2,1)S(1)}, u32[]{:S(2)}) %copy-start.2) | copy-done | bytes 65560
  24.6 1.8 %regroup.1.refs_0_ = bf16[4,128,256]{2,1,0:T(8,128)(2,1)} custom-call(bf16[4,64,128]{2,1,0:T(8,128)(2,1)} %get-tuple-element.6.refs_0_, bf16[4,64,128]{2,1,0:T(8,128)(2,1)} %copy-done, bf16[4,64,128]{2,1,0:T(8,128)(2,1)} %copy-done.1, bf16[4,64,128]{2,1,0:T(8,128)(2,1)} %copy-done.2), custom_call_target="tpu_custom_call" | custom-call | tf_op jit(solution)/shard_map/regroup/pallas_call | solution.py:167
  26.4 1.3 %collective-permute-start.4 = (bf16[4,128,256]{2,1,0:T(8,128)(2,1)}, bf16[4,128,256]{2,1,0:T(8,128)(2,1)S(1)}, u32[]{:S(2)}, u32[]{:S(2)}) collective-permute-start(bf16[4,128,256]{2,1,0:T(8,128)(2,1)} %regroup.1.refs_0_), channel_id=1, source_target_pairs={{0,2},{2,0},{1,3},{3,1},{4,6},{6,4},{5,7},{7,5},{8,10},{10,8},{9,1... | collective-permute-start | bytes 786440 | tf_op jit(solution)/shard_map/ppermute | solution.py:254
  27.7 3.1 %collective-permute-start.7 = (bf16[4,128,256]{2,1,0:T(8,128)(2,1)}, bf16[4,128,256]{2,1,0:T(8,128)(2,1)S(1)}, u32[]{:S(2)}, u32[]{:S(2)}) collective-permute-start(bf16[4,128,256]{2,1,0:T(8,128)(2,1)} %regroup.1.refs_0_), channel_id=1, source_target_pairs={{1,4},{3,5},{5,2},{7,3},{9,12},{11,13},{13,10},{15,11},{17,20},{19... | collective-permute-start | bytes 786440 | tf_op jit(solution)/shard_map/ppermute | solution.py:256
  30.8 1.3 %collective-permute-start.6 = (bf16[4,128,256]{2,1,0:T(8,128)(2,1)}, bf16[4,128,256]{2,1,0:T(8,128)(2,1)S(1)}, u32[]{:S(2)}, u32[]{:S(2)}) collective-permute-start(bf16[4,128,256]{2,1,0:T(8,128)(2,1)} %regroup.1.refs_0_), channel_id=1, source_target_pairs={{0,4},{2,5},{4,2},{6,3},{8,12},{10,13},{12,10},{14,11},{16,20},{18... | collective-permute-start | bytes 786440 | tf_op jit(solution)/shard_map/ppermute | solution.py:256
  32.1 0.5 collective-permute-start.3
  32.5 3.9 %collective-permute-done.4.refs_2_ = bf16[4,128,256]{2,1,0:T(8,128)(2,1)S(1)} collective-permute-done((bf16[4,128,256]{2,1,0:T(8,128)(2,1)}, bf16[4,128,256]{2,1,0:T(8,128)(2,1)S(1)}, u32[]{:S(2)}, u32[]{:S(2)}) %collective-permute-start.4) | collective-permute-done | bytes 262176 | tf_op jit(solution)/shard_map/ppermute | solution.py:254
  36.4 0.0 copy-start.3
  36.4 4.5 %collective-permute-start.5 = (bf16[4,128,256]{2,1,0:T(8,128)(2,1)S(1)}, bf16[4,128,256]{2,1,0:T(8,128)(2,1)S(1)}, u32[]{:S(2)}, u32[]{:S(2)}) collective-permute-start(bf16[4,128,256]{2,1,0:T(8,128)(2,1)S(1)} %collective-permute-done.4.refs_2_), channel_id=1, source_target_pairs={{0,1},{1,0},{2,3},{3,2},{4,5},{5,4},{6,7},{7,6},{8,9},{9,8},{10,11... | collective-permute-start | bytes 786440 | tf_op jit(solution)/shard_map/ppermute | solution.py:264
  41.0 0.0 collective-permute-done.7.refs_5_
  41.0 0.0 copy-start.4
  41.0 0.0 collective-permute-done.6.refs_4_
  41.0 0.0 copy-start.5
  41.0 0.0 collective-permute-done.3.refs_1_
  41.0 0.0 copy-start.6
  41.0 1.1 %collective-permute-done.5.refs_3_ = bf16[4,128,256]{2,1,0:T(8,128)(2,1)S(1)} collective-permute-done((bf16[4,128,256]{2,1,0:T(8,128)(2,1)S(1)}, bf16[4,128,256]{2,1,0:T(8,128)(2,1)S(1)}, u32[]{:S(2)}, u32[]{:S(2)}) %collective-permute-start.5) | collective-permute-done | bytes 262176 | tf_op jit(solution)/shard_map/ppermute | solution.py:264
  42.1 0.0 copy-done.3
  42.1 0.0 copy-done.4
  42.1 0.0 copy-done.5
  42.1 0.0 copy-done.6
  42.1 0.0 copy-start.7
  42.2 0.7 %copy-done.7 = bf16[4,128,256]{2,1,0:T(8,128)(2,1)} copy-done((bf16[4,128,256]{2,1,0:T(8,128)(2,1)}, bf16[4,128,256]{2,1,0:T(8,128)(2,1)S(1)}, u32[]{:S(2)}) %copy-start.7) | copy-done | bytes 262168
  42.9 6.4 %products.1 = (bf16[4,1024,512]{2,1,0:T(8,128)(2,1)}, bf16[4,1024,512]{2,1,0:T(8,128)(2,1)}) custom-call(bf16[4,128,256]{2,1,0:T(8,128)(2,1)} %regroup.1.refs_0_, bf16[4,128,256]{2,1,0:T(8,128)(2,1)} %copy-done.6, bf16[4,128,256]{2,1,0:T(8,128)(2,1)} %copy-done.3, bf16[4,128,256]{2,1,0:T(8,128)(2,1)} %copy-done.7, bf16[4,128,256]{2,1,0:T(8,128)(2,1)} %copy-done.5, ...), custom_call_target="tpu_custom_call" | custom-call | flops 1073741824 | bytes 8388608 | tf_op jit(solution)/shard_map/products/pallas_call | solution.py:224
Async XLA Ops:
  15.0 3.8 %collective-permute-start = (bf16[4,64,128]{2,1,0:T(8,128)(2,1)}, bf16[4,64,128]{2,1,0:T(8,128)(2,1)S(1)}, u32[]{:S(2)}, u32[]{:S(2)}) collective-permute-start(bf16[4,64,128]{2,1,0:T(8,128)(2,1)} %get-tuple-element.7), channel_id=1, source_target_pairs={{0,8},{8,16},{16,24},{24,0},{1,9},{9,17},{17,25},{25,1},{2,10},{10... | collective-permute-start | bytes 196616 | tf_op jit(solution)/shard_map/ppermute | solution.py:246
  16.3 4.6 %collective-permute-start.1 = (bf16[4,64,128]{2,1,0:T(8,128)(2,1)}, bf16[4,64,128]{2,1,0:T(8,128)(2,1)S(1)}, u32[]{:S(2)}, u32[]{:S(2)}) collective-permute-start(bf16[4,64,128]{2,1,0:T(8,128)(2,1)} %get-tuple-element.8), channel_id=1, source_target_pairs={{0,16},{8,24},{16,0},{24,8},{1,17},{9,25},{17,1},{25,9},{2,18},{10... | collective-permute-start | bytes 196616 | tf_op jit(solution)/shard_map/ppermute | solution.py:246
  17.4 6.6 %collective-permute-start.2 = (bf16[4,64,128]{2,1,0:T(8,128)(2,1)}, bf16[4,64,128]{2,1,0:T(8,128)(2,1)S(1)}, u32[]{:S(2)}, u32[]{:S(2)}) collective-permute-start(bf16[4,64,128]{2,1,0:T(8,128)(2,1)} %get-tuple-element.9), channel_id=1, source_target_pairs={{0,24},{8,0},{16,8},{24,16},{1,25},{9,1},{17,9},{25,17},{2,26},{10... | collective-permute-start | bytes 196616 | tf_op jit(solution)/shard_map/ppermute | solution.py:246
  18.8 5.2 %copy-start = (bf16[4,64,128]{2,1,0:T(8,128)(2,1)}, bf16[4,64,128]{2,1,0:T(8,128)(2,1)S(1)}, u32[]{:S(2)}) copy-start(bf16[4,64,128]{2,1,0:T(8,128)(2,1)S(1)} %collective-permute-done.refs_1_) | copy-start | bytes 196612
  21.0 3.0 %copy-start.1 = (bf16[4,64,128]{2,1,0:T(8,128)(2,1)}, bf16[4,64,128]{2,1,0:T(8,128)(2,1)S(1)}, u32[]{:S(2)}) copy-start(bf16[4,64,128]{2,1,0:T(8,128)(2,1)S(1)} %collective-permute-done.1.refs_2_) | copy-start | bytes 196612
  24.0 0.6 %copy-start.2 = (bf16[4,64,128]{2,1,0:T(8,128)(2,1)}, bf16[4,64,128]{2,1,0:T(8,128)(2,1)S(1)}, u32[]{:S(2)}) copy-start(bf16[4,64,128]{2,1,0:T(8,128)(2,1)S(1)} %collective-permute-done.2.refs_3_) | copy-start | bytes 196612
  26.4 10.0 %collective-permute-start.4 = (bf16[4,128,256]{2,1,0:T(8,128)(2,1)}, bf16[4,128,256]{2,1,0:T(8,128)(2,1)S(1)}, u32[]{:S(2)}, u32[]{:S(2)}) collective-permute-start(bf16[4,128,256]{2,1,0:T(8,128)(2,1)} %regroup.1.refs_0_), channel_id=1, source_target_pairs={{0,2},{2,0},{1,3},{3,1},{4,6},{6,4},{5,7},{7,5},{8,10},{10,8},{9,1... | collective-permute-start | bytes 786440 | tf_op jit(solution)/shard_map/ppermute | solution.py:254
  27.7 13.3 %collective-permute-start.7 = (bf16[4,128,256]{2,1,0:T(8,128)(2,1)}, bf16[4,128,256]{2,1,0:T(8,128)(2,1)S(1)}, u32[]{:S(2)}, u32[]{:S(2)}) collective-permute-start(bf16[4,128,256]{2,1,0:T(8,128)(2,1)} %regroup.1.refs_0_), channel_id=1, source_target_pairs={{1,4},{3,5},{5,2},{7,3},{9,12},{11,13},{13,10},{15,11},{17,20},{19... | collective-permute-start | bytes 786440 | tf_op jit(solution)/shard_map/ppermute | solution.py:256
  30.8 10.2 %collective-permute-start.6 = (bf16[4,128,256]{2,1,0:T(8,128)(2,1)}, bf16[4,128,256]{2,1,0:T(8,128)(2,1)S(1)}, u32[]{:S(2)}, u32[]{:S(2)}) collective-permute-start(bf16[4,128,256]{2,1,0:T(8,128)(2,1)} %regroup.1.refs_0_), channel_id=1, source_target_pairs={{0,4},{2,5},{4,2},{6,3},{8,12},{10,13},{12,10},{14,11},{16,20},{18... | collective-permute-start | bytes 786440 | tf_op jit(solution)/shard_map/ppermute | solution.py:256
  32.1 8.9 %collective-permute-start.3 = (bf16[4,128,256]{2,1,0:T(8,128)(2,1)}, bf16[4,128,256]{2,1,0:T(8,128)(2,1)S(1)}, u32[]{:S(2)}, u32[]{:S(2)}) collective-permute-start(bf16[4,128,256]{2,1,0:T(8,128)(2,1)} %regroup.1.refs_0_), channel_id=1, source_target_pairs={{0,1},{1,0},{2,3},{3,2},{4,5},{5,4},{6,7},{7,6},{8,9},{9,8},{10,11... | collective-permute-start | bytes 786440 | tf_op jit(solution)/shard_map/ppermute | solution.py:263
  36.4 5.7 %copy-start.3 = (bf16[4,128,256]{2,1,0:T(8,128)(2,1)}, bf16[4,128,256]{2,1,0:T(8,128)(2,1)S(1)}, u32[]{:S(2)}) copy-start(bf16[4,128,256]{2,1,0:T(8,128)(2,1)S(1)} %collective-permute-done.4.refs_2_) | copy-start | bytes 786436
  36.4 5.7 %collective-permute-start.5 = (bf16[4,128,256]{2,1,0:T(8,128)(2,1)S(1)}, bf16[4,128,256]{2,1,0:T(8,128)(2,1)S(1)}, u32[]{:S(2)}, u32[]{:S(2)}) collective-permute-start(bf16[4,128,256]{2,1,0:T(8,128)(2,1)S(1)} %collective-permute-done.4.refs_2_), channel_id=1, source_target_pairs={{0,1},{1,0},{2,3},{3,2},{4,5},{5,4},{6,7},{7,6},{8,9},{9,8},{10,11... | collective-permute-start | bytes 786440 | tf_op jit(solution)/shard_map/ppermute | solution.py:264
  41.0 1.2 %copy-start.4 = (bf16[4,128,256]{2,1,0:T(8,128)(2,1)}, bf16[4,128,256]{2,1,0:T(8,128)(2,1)S(1)}, u32[]{:S(2)}) copy-start(bf16[4,128,256]{2,1,0:T(8,128)(2,1)S(1)} %collective-permute-done.7.refs_5_) | copy-start | bytes 786436
  41.0 1.2 %copy-start.5 = (bf16[4,128,256]{2,1,0:T(8,128)(2,1)}, bf16[4,128,256]{2,1,0:T(8,128)(2,1)S(1)}, u32[]{:S(2)}) copy-start(bf16[4,128,256]{2,1,0:T(8,128)(2,1)S(1)} %collective-permute-done.6.refs_4_) | copy-start | bytes 786436
  41.0 1.1 %copy-start.6 = (bf16[4,128,256]{2,1,0:T(8,128)(2,1)}, bf16[4,128,256]{2,1,0:T(8,128)(2,1)S(1)}, u32[]{:S(2)}) copy-start(bf16[4,128,256]{2,1,0:T(8,128)(2,1)S(1)} %collective-permute-done.3.refs_1_) | copy-start | bytes 786436
  42.1 0.7 %copy-start.7 = (bf16[4,128,256]{2,1,0:T(8,128)(2,1)}, bf16[4,128,256]{2,1,0:T(8,128)(2,1)S(1)}, u32[]{:S(2)}) copy-start(bf16[4,128,256]{2,1,0:T(8,128)(2,1)S(1)} %collective-permute-done.5.refs_3_) | copy-start | bytes 786436

commit v2 on v1

--- a/solution.py
+++ b/solution.py
@@ -14,7 +14,19 @@
 SPEC = 64
 CH_DEV = 4
 LANES = 128
+AHEAD = 3
 VMEM_BYTES = 60 * 2**20
+
+
+SHIFTS = (0, 2, 1, 3)
+
+
+def partner(me, s, groups, sign=1):
+    return lax.rem(me + sign * SHIFTS[s] + groups, groups)
+
+
+def target_of(i, s, groups):
+    return (i + SHIFTS[s]) % groups
 
 
 def dft_rows(channels):
@@ -31,24 +43,36 @@
 
 
 def channelize_body(
-    gain_ref, taps_ref, table_ref, samples_ref, *rest, first, half, blocks, groups
+    gain_hbm, taps_hbm, table_hbm, samples_ref, *rest, first, half, blocks, groups
 ):
-    outs, (weights, raw, lhs, sums, held, sems) = rest[:groups], rest[groups:]
+    outs, scratch = rest[:groups], rest[groups:]
+    gain_ref, taps_ref, table_ref, weights, raw, lhs, sums, held, sems, small_sems = scratch
     inputs = samples_ref.shape[1]
     rows = table_ref.shape[0]
-    pieces = []
+    small = [
+        pltpu.make_async_copy(source, target, small_sems.at[index])
+        for index, (source, target) in enumerate(
+            [(taps_hbm, taps_ref), (table_hbm, table_ref), (gain_hbm, gain_ref)]
+        )
+    ]
+    for copy in small:
+        copy.start()
+    copies = []
     for index, (start, stop) in enumerate(blocks):
-        pieces.append((index, 0, start, min(stop, half)))
-        pieces.append((index, 1, half + start, half + stop))
-    copies = {}
-    for index, side, begin, end in pieces:
-        if begin < end:
-            span = pl.ds(begin * NFFT, (end - begin) * NFFT)
-            source = pl.ds((first + begin) * NFFT, (end - begin) * NFFT)
-            copies[index, side] = pltpu.make_async_copy(
-                samples_ref.at[:, :, source], raw.at[:, :, span], sems.at[index, side]
-            )
-            copies[index, side].start()
+        copies.append([])
+        for side, begin, end in ((0, start, min(stop, half)), (1, half + start, half + stop)):
+            if begin < end:
+                span = pl.ds(begin * NFFT, (end - begin) * NFFT)
+                source = pl.ds((first + begin) * NFFT, (end - begin) * NFFT)
+                copy = pltpu.make_async_copy(
+                    samples_ref.at[:, :, source], raw.at[:, :, span], sems.at[index, side]
+                )
+                copies[-1].append(copy)
+    for index in range(min(AHEAD, len(blocks))):
+        for copy in copies[index]:
+            copy.start()
+    for copy in small:
+        copy.wait()
     for p in range(2):
         for b in range(NFFT // LANES):
             table = table_ref[:, p * NFFT + b * LANES : p * NFFT + (b + 1) * LANES].astype(
@@ -61,10 +85,14 @@
                 at = pl.ds(p * NFFT + b * LANES, LANES)
                 weights[t * rows : (t + 1) * rows, at] = high
                 weights[(TAPS + t) * rows : (TAPS + t + 1) * rows, at] = low
+    gain = gain_ref[...]
+    gain = jnp.concatenate([gain, gain], axis=1) * (0.25 / math.sqrt(SPEC))
     for index, (start, stop) in enumerate(blocks):
-        for side in range(2):
-            if (index, side) in copies:
-                copies[index, side].wait()
+        for copy in copies[index]:
+            copy.wait()
+        if index + AHEAD < len(blocks):
+            for copy in copies[index + AHEAD]:
+                copy.start()
         buffer = lhs[index % 2]
         for slot in range(start, stop):
             for side in range(2):
@@ -84,19 +112,17 @@
             preferred_element_type=jnp.float32,
         )
         sums[:, start * LANES : stop * LANES] = both[: TAPS * rows] + both[TAPS * rows :]
-    gain = gain_ref[...]
-    gain = jnp.concatenate([gain, gain], axis=1) * (0.25 / math.sqrt(SPEC))
-    for slot in range(half):
-        total = sums[0:rows, slot * LANES : (slot + 1) * LANES]
-        for t in range(1, TAPS):
-            total = total + sums[
-                t * rows : (t + 1) * rows, (slot + t) * LANES : (slot + t + 1) * LANES
-            ]
-        held[pl.ds(slot, rows, stride=half), :] = total * gain
+        for slot in range(max(start - TAPS + 1, 0), stop - TAPS + 1):
+            total = sums[0:rows, slot * LANES : (slot + 1) * LANES]
+            for t in range(1, TAPS):
+                total = total + sums[
+                    t * rows : (t + 1) * rows, (slot + t) * LANES : (slot + t + 1) * LANES
+                ]
+            held[pl.ds(slot, rows, stride=half), :] = total * gain
     me = lax.axis_index("freq")
     depth = 2 * half
     for s in range(groups):
-        to = lax.rem(me + s, groups) * (CH_DEV * depth)
+        to = partner(me, s, groups) * (CH_DEV * depth)
         for k in range(CH_DEV):
             outs[s][k] = held[
                 pl.ds(pl.multiple_of(to + k * depth, 8), depth), :
@@ -115,22 +141,20 @@
         functools.partial(
             channelize_body, first=first, half=half, blocks=blocks, groups=groups
         ),
-        grid=(1,),
-        in_specs=[
-            pl.BlockSpec((1, inputs), lambda i: (0, 0)),
-            pl.BlockSpec((TAPS, NFFT), lambda i: (0, 0)),
-            pl.BlockSpec((rows, 2 * NFFT), lambda i: (0, 0)),
-            pl.BlockSpec(memory_space=pl.ANY),
-        ],
-        out_specs=[pl.BlockSpec((CH_DEV, 2 * half, LANES), lambda i: (0, 0, 0))] * groups,
+        in_specs=[pl.BlockSpec(memory_space=pltpu.HBM)] * 4,
+        out_specs=[pl.BlockSpec(memory_space=pltpu.VMEM)] * groups,
         out_shape=[jax.ShapeDtypeStruct((CH_DEV, 2 * half, LANES), jnp.bfloat16)] * groups,
         scratch_shapes=[
+            pltpu.VMEM((1, inputs), jnp.float32),
+            pltpu.VMEM((TAPS, NFFT), jnp.float32),
+            pltpu.VMEM((rows, 2 * NFFT), jnp.bfloat16),
             pltpu.VMEM((2 * TAPS * rows, 2 * NFFT), jnp.bfloat16),
             pltpu.VMEM((2, inputs, frames * NFFT), jnp.int32),
             [pltpu.VMEM((widest * 2 * inputs, 2 * NFFT), jnp.bfloat16)] * 2,
             pltpu.VMEM((TAPS * rows, slots * LANES), jnp.float32),
             pltpu.VMEM((rows * half, LANES), jnp.float32),
             pltpu.SemaphoreType.DMA((len(blocks), 2)),
+            pltpu.SemaphoreType.DMA((3,)),
         ],
         compiler_params=pltpu.CompilerParams(vmem_limit_bytes=VMEM_BYTES),
         cost_estimate=pl.CostEstimate(
@@ -147,7 +171,7 @@
     sources, out, ordered = refs[:groups], refs[groups], refs[groups + 1]
     me = lax.axis_index("freq")
     for s in range(groups):
-        ordered[lax.rem(me - s + groups, groups)] = sources[s][...]
+        ordered[partner(me, s, groups, -1)] = sources[s][...]
     depth = 2 * half
     lane = lax.broadcasted_iota(jnp.int32, (depth, LANES), 1)
     for pair in range(groups // 2):
@@ -168,6 +192,7 @@
         functools.partial(regroup_body, half=half),
         out_shape=jax.ShapeDtypeStruct(shape, jnp.bfloat16),
         scratch_shapes=[pltpu.VMEM((groups,) + sources[0].shape, jnp.bfloat16)],
+        compiler_params=pltpu.CompilerParams(vmem_limit_bytes=4 * 2**20),
         name="regroup",
     )(*sources)
 
@@ -231,7 +256,7 @@
             pltpu.VMEM((4, parts * deep, width), jnp.bfloat16),
             pltpu.VMEM((parts * deep, 4 * width), jnp.bfloat16),
         ],
-        compiler_params=pltpu.CompilerParams(vmem_limit_bytes=VMEM_BYTES),
+        compiler_params=pltpu.CompilerParams(vmem_limit_bytes=24 * 2**20),
         cost_estimate=pl.CostEstimate(
             flops=2 * CH_DEV * parts * deep * 16 * width * width,
             bytes_accessed=2 * 2 * CH_DEV * 8 * width * width,
@@ -242,9 +267,8 @@
 
 
 def exchange(sent, groups):
-    ring = lambda s: [(i, (i + s) % groups) for i in range(groups)]
-    turned = [sent[0]] + [lax.ppermute(sent[s], "freq", ring(s)) for s in range(1, groups)]
-    return turned
+    moves = [[(i, target_of(i, s, groups)) for i in range(groups)] for s in range(groups)]
+    return [sent[0]] + [lax.ppermute(sent[s], "freq", moves[s]) for s in range(1, groups)]
 
 
 def gather(mine):

time: 49.7 us -> 44.5 us (0.90)
  Pallas kernels: 22.6 us -> 18.7 us
  starting transfers between devices: 14.4 us -> 13.6 us
  local copies, waits for them, and re-layouts: 1.35 us -> 0.84 us
    pallas_call x1, Pallas kernels: 1.8 us -> 0.16 us  [regroup(): pl.pallas_call(functools.partial(regroup_body, half=half), out_shape=jax....]
    pallas_call x1, Pallas kernels: 6.42 us -> 4.79 us  [products(): pl.pallas_call(functools.partial(products_body, half=half, parts=parts),...]
    ppermute x1, waiting for transfers between devices: 3.93 us -> 4.59 us  [gather(): far_y = lax.ppermute(mine, 'col', other_y)]
    pallas_call x1, Pallas kernels: 14.4 us -> 13.7 us  [channelize(): pl.pallas_call(functools.partial(channelize_body, first=first, half=half,...]
    unnamed x16 -> x2, local copies, waits for them, and re-layouts: 1.35 us -> 0.84 us
  transfers between devices with their start and end apart: 8 -> 8, of which waited for: 4 -> 5; matrix products, arithmetic and copies ran while one was open for 0% -> 0% of each run, Pallas kernels for 0% -> 0%
where the time goes in v2:
time: 44.5 us; the launch traced here: 44.3 us
  Pallas kernels  18.7 us (42%)
  starting transfers between devices  13.6 us (31%)
  waiting for transfers between devices  10.5 us (24%)
  local copies, waits for them, and re-layouts  0.84 us (2%)
  between operations  0.67 us (2%)
    pallas_call x1, Pallas kernels, channelize(): pl.pallas_call(functools.partial(channelize_body, first=first, half=half,...  13.7 us
    pallas_call x1, Pallas kernels, products(): pl.pallas_call(functools.partial(products_body, half=half, parts=parts),...  4.79 us
    ppermute x3, waiting for transfers between devices, exchange(): lax.ppermute(sent[s], 'freq', moves[s])  4.72 us
    ppermute x1, waiting for transfers between devices, gather(): far_y = lax.ppermute(mine, 'col', other_y)  4.59 us
    ppermute x1, starting transfers between devices, gather(): far = lax.ppermute(far_y, 'col', other_core)  4.07 us
    ppermute x2, starting transfers between devices, gather(): lax.ppermute(mine, ('row', 'col'), [(place(x, y, c), place(1 - x, x, y))...  3.97 us
    ppermute x3, starting transfers between devices, exchange(): lax.ppermute(sent[s], 'freq', moves[s])  3.83 us
    ppermute x1, starting transfers between devices, gather(): far_y = lax.ppermute(mine, 'col', other_y)  1.3 us
  transfers between devices with their start and end apart: 8, of which 5 were waited for; matrix products, arithmetic and copies ran while one was open for 0% of the time, Pallas kernels for 0%

profile of v2, /device:TPU:11, one launch (start us, length us, event | category | flops | bytes accessed | tf_op | source)
XLA Modules:
  0.0 44.3 jit_solution(2188105605966357567)
XLA Ops:
  0.6 13.7 %channelize.1 = (bf16[4,64,128]{2,1,0:T(8,128)(2,1)}, bf16[4,64,128]{2,1,0:T(8,128)(2,1)}, bf16[4,64,128]{2,1,0:T(8,128)(2,1)}, bf16[4,64,128]{2,1,0:T(8,128)(2,1)}) custom-call(f32[1,64]{1,0:T(1,128)} %bitcast.1, f32[4,1024]{1,0:T(4,128)} %taps_hbm.1, bf16[32,2048]{1,0:T(8,128)(2,1)} %constant.3.table_hbm, s32[2,64,68608]{2,1,0:T(8,128)} %samples_ref.1), custom_call_target="tpu_custom_call" | custom-call | flops 4496293888 | bytes 35127296 | tf_op jit(solution)/shard_map/channelize/pallas_call | solution.py:140
  14.4 2.4 %collective-permute-start = (bf16[4,64,128]{2,1,0:T(8,128)(2,1)}, bf16[4,64,128]{2,1,0:T(8,128)(2,1)S(1)}, u32[]{:S(2)}, u32[]{:S(2)}) collective-permute-start(bf16[4,64,128]{2,1,0:T(8,128)(2,1)} %get-tuple-element.7), channel_id=1, source_target_pairs={{0,16},{8,24},{16,0},{24,8},{1,17},{9,25},{17,1},{25,9},{2,18},{10... | collective-permute-start | bytes 196616 | tf_op jit(solution)/shard_map/ppermute | solution.py:271
  16.7 0.0 collective-permute-start.1
  16.7 1.5 %collective-permute-start.2 = (bf16[4,64,128]{2,1,0:T(8,128)(2,1)}, bf16[4,64,128]{2,1,0:T(8,128)(2,1)S(1)}, u32[]{:S(2)}, u32[]{:S(2)}) collective-permute-start(bf16[4,64,128]{2,1,0:T(8,128)(2,1)} %get-tuple-element.9), channel_id=1, source_target_pairs={{0,24},{8,0},{16,8},{24,16},{1,25},{9,1},{17,9},{25,17},{2,26},{10... | collective-permute-start | bytes 196616 | tf_op jit(solution)/shard_map/ppermute | solution.py:271
  18.2 1.1 %collective-permute-done.refs_1_ = bf16[4,64,128]{2,1,0:T(8,128)(2,1)S(1)} collective-permute-done((bf16[4,64,128]{2,1,0:T(8,128)(2,1)}, bf16[4,64,128]{2,1,0:T(8,128)(2,1)S(1)}, u32[]{:S(2)}, u32[]{:S(2)}) %collective-permute-start) | collective-permute-done | bytes 65568 | tf_op jit(solution)/shard_map/ppermute | solution.py:271
  19.3 2.0 %collective-permute-done.1.refs_2_ = bf16[4,64,128]{2,1,0:T(8,128)(2,1)S(1)} collective-permute-done((bf16[4,64,128]{2,1,0:T(8,128)(2,1)}, bf16[4,64,128]{2,1,0:T(8,128)(2,1)S(1)}, u32[]{:S(2)}, u32[]{:S(2)}) %collective-permute-start.1) | collective-permute-done | bytes 65568 | tf_op jit(solution)/shard_map/ppermute | solution.py:271
  21.3 1.6 %collective-permute-done.2.refs_3_ = bf16[4,64,128]{2,1,0:T(8,128)(2,1)S(1)} collective-permute-done((bf16[4,64,128]{2,1,0:T(8,128)(2,1)}, bf16[4,64,128]{2,1,0:T(8,128)(2,1)S(1)}, u32[]{:S(2)}, u32[]{:S(2)}) %collective-permute-start.2) | collective-permute-done | bytes 65568 | tf_op jit(solution)/shard_map/ppermute | solution.py:271
  22.9 0.0 copy-start
  22.9 0.8 %copy-done = bf16[4,64,128]{2,1,0:T(8,128)(2,1)S(1)} copy-done((bf16[4,64,128]{2,1,0:T(8,128)(2,1)S(1)}, bf16[4,64,128]{2,1,0:T(8,128)(2,1)}, u32[]{:S(2)}) %copy-start) | copy-done | bytes 65560
  23.8 0.2 regroup.1.refs_0_
  23.9 1.3 %collective-permute-start.4 = (bf16[4,128,256]{2,1,0:T(8,128)(2,1)S(1)}, bf16[4,128,256]{2,1,0:T(8,128)(2,1)S(1)}, u32[]{:S(2)}, u32[]{:S(2)}) collective-permute-start(bf16[4,128,256]{2,1,0:T(8,128)(2,1)S(1)} %regroup.1.refs_0_), channel_id=1, source_target_pairs={{0,2},{2,0},{1,3},{3,1},{4,6},{6,4},{5,7},{7,5},{8,10},{10,8},{9,1... | collective-permute-start | bytes 786440 | tf_op jit(solution)/shard_map/ppermute | solution.py:278
  25.2 2.7 %collective-permute-start.7 = (bf16[4,128,256]{2,1,0:T(8,128)(2,1)S(1)}, bf16[4,128,256]{2,1,0:T(8,128)(2,1)S(1)}, u32[]{:S(2)}, u32[]{:S(2)}) collective-permute-start(bf16[4,128,256]{2,1,0:T(8,128)(2,1)S(1)} %regroup.1.refs_0_), channel_id=1, source_target_pairs={{1,4},{3,5},{5,2},{7,3},{9,12},{11,13},{13,10},{15,11},{17,20},{19... | collective-permute-start | bytes 786440 | tf_op jit(solution)/shard_map/ppermute | solution.py:280
  27.9 1.3 %collective-permute-start.6 = (bf16[4,128,256]{2,1,0:T(8,128)(2,1)S(1)}, bf16[4,128,256]{2,1,0:T(8,128)(2,1)S(1)}, u32[]{:S(2)}, u32[]{:S(2)}) collective-permute-start(bf16[4,128,256]{2,1,0:T(8,128)(2,1)S(1)} %regroup.1.refs_0_), channel_id=1, source_target_pairs={{0,4},{2,5},{4,2},{6,3},{8,12},{10,13},{12,10},{14,11},{16,20},{18... | collective-permute-start | bytes 786440 | tf_op jit(solution)/shard_map/ppermute | solution.py:280
  29.2 0.5 %collective-permute-start.3 = (bf16[4,128,256]{2,1,0:T(8,128)(2,1)S(1)}, bf16[4,128,256]{2,1,0:T(8,128)(2,1)S(1)}, u32[]{:S(2)}, u32[]{:S(2)}) collective-permute-start(bf16[4,128,256]{2,1,0:T(8,128)(2,1)S(1)} %regroup.1.refs_0_), channel_id=1, source_target_pairs={{0,1},{1,0},{2,3},{3,2},{4,5},{5,4},{6,7},{7,6},{8,9},{9,8},{10,11... | collective-permute-start | bytes 786440 | tf_op jit(solution)/shard_map/ppermute | solution.py:287
  29.7 4.6 %collective-permute-done.4.refs_2_ = bf16[4,128,256]{2,1,0:T(8,128)(2,1)S(1)} collective-permute-done((bf16[4,128,256]{2,1,0:T(8,128)(2,1)S(1)}, bf16[4,128,256]{2,1,0:T(8,128)(2,1)S(1)}, u32[]{:S(2)}, u32[]{:S(2)}) %collective-permute-start.4) | collective-permute-done | bytes 262176 | tf_op jit(solution)/shard_map/ppermute | solution.py:278
  34.3 4.1 %collective-permute-start.5 = (bf16[4,128,256]{2,1,0:T(8,128)(2,1)S(1)}, bf16[4,128,256]{2,1,0:T(8,128)(2,1)S(1)}, u32[]{:S(2)}, u32[]{:S(2)}) collective-permute-start(bf16[4,128,256]{2,1,0:T(8,128)(2,1)S(1)} %collective-permute-done.4.refs_2_), channel_id=1, source_target_pairs={{0,1},{1,0},{2,3},{3,2},{4,5},{5,4},{6,7},{7,6},{8,9},{9,8},{10,11... | collective-permute-start | bytes 786440 | tf_op jit(solution)/shard_map/ppermute | solution.py:288
  38.3 0.0 collective-permute-done.7.refs_5_
  38.3 0.0 collective-permute-done.6.refs_4_
  38.3 0.0 collective-permute-done.3.refs_1_
  38.3 1.1 %collective-permute-done.5.refs_3_ = bf16[4,128,256]{2,1,0:T(8,128)(2,1)S(1)} collective-permute-done((bf16[4,128,256]{2,1,0:T(8,128)(2,1)S(1)}, bf16[4,128,256]{2,1,0:T(8,128)(2,1)S(1)}, u32[]{:S(2)}, u32[]{:S(2)}) %collective-permute-start.5) | collective-permute-done | bytes 262176 | tf_op jit(solution)/shard_map/ppermute | solution.py:288
  39.5 4.8 %products.1 = (bf16[4,1024,512]{2,1,0:T(8,128)(2,1)}, bf16[4,1024,512]{2,1,0:T(8,128)(2,1)}) custom-call(bf16[4,128,256]{2,1,0:T(8,128)(2,1)S(1)} %regroup.1.refs_0_, bf16[4,128,256]{2,1,0:T(8,128)(2,1)S(1)} %collective-permute-done.3.refs_1_, bf16[4,128,256]{2,1,0:T(8,128)(2,1)S(1)} %collective-permute-done.4.refs_2_, ...), custom_call_target="tpu_custom_call" | custom-call | flops 1073741824 | bytes 8388608 | tf_op jit(solution)/shard_map/products/pallas_call | solution.py:249
Async XLA Ops:
  14.4 4.9 %collective-permute-start = (bf16[4,64,128]{2,1,0:T(8,128)(2,1)}, bf16[4,64,128]{2,1,0:T(8,128)(2,1)S(1)}, u32[]{:S(2)}, u32[]{:S(2)}) collective-permute-start(bf16[4,64,128]{2,1,0:T(8,128)(2,1)} %get-tuple-element.7), channel_id=1, source_target_pairs={{0,16},{8,24},{16,0},{24,8},{1,17},{9,25},{17,1},{25,9},{2,18},{10... | collective-permute-start | bytes 196616 | tf_op jit(solution)/shard_map/ppermute | solution.py:271
  16.7 4.6 %collective-permute-start.1 = (bf16[4,64,128]{2,1,0:T(8,128)(2,1)}, bf16[4,64,128]{2,1,0:T(8,128)(2,1)S(1)}, u32[]{:S(2)}, u32[]{:S(2)}) collective-permute-start(bf16[4,64,128]{2,1,0:T(8,128)(2,1)} %get-tuple-element.8), channel_id=1, source_target_pairs={{0,8},{8,16},{16,24},{24,0},{1,9},{9,17},{17,25},{25,1},{2,10},{10... | collective-permute-start | bytes 196616 | tf_op jit(solution)/shard_map/ppermute | solution.py:271
  16.7 6.2 %collective-permute-start.2 = (bf16[4,64,128]{2,1,0:T(8,128)(2,1)}, bf16[4,64,128]{2,1,0:T(8,128)(2,1)S(1)}, u32[]{:S(2)}, u32[]{:S(2)}) collective-permute-start(bf16[4,64,128]{2,1,0:T(8,128)(2,1)} %get-tuple-element.9), channel_id=1, source_target_pairs={{0,24},{8,0},{16,8},{24,16},{1,25},{9,1},{17,9},{25,17},{2,26},{10... | collective-permute-start | bytes 196616 | tf_op jit(solution)/shard_map/ppermute | solution.py:271
  22.9 0.8 %copy-start = (bf16[4,64,128]{2,1,0:T(8,128)(2,1)S(1)}, bf16[4,64,128]{2,1,0:T(8,128)(2,1)}, u32[]{:S(2)}) copy-start(bf16[4,64,128]{2,1,0:T(8,128)(2,1)} %get-tuple-element.6.refs_0_) | copy-start | bytes 196612
  23.9 10.3 %collective-permute-start.4 = (bf16[4,128,256]{2,1,0:T(8,128)(2,1)S(1)}, bf16[4,128,256]{2,1,0:T(8,128)(2,1)S(1)}, u32[]{:S(2)}, u32[]{:S(2)}) collective-permute-start(bf16[4,128,256]{2,1,0:T(8,128)(2,1)S(1)} %regroup.1.refs_0_), channel_id=1, source_target_pairs={{0,2},{2,0},{1,3},{3,1},{4,6},{6,4},{5,7},{7,5},{8,10},{10,8},{9,1... | collective-permute-start | bytes 786440 | tf_op jit(solution)/shard_map/ppermute | solution.py:278
  25.2 13.1 %collective-permute-start.7 = (bf16[4,128,256]{2,1,0:T(8,128)(2,1)S(1)}, bf16[4,128,256]{2,1,0:T(8,128)(2,1)S(1)}, u32[]{:S(2)}, u32[]{:S(2)}) collective-permute-start(bf16[4,128,256]{2,1,0:T(8,128)(2,1)S(1)} %regroup.1.refs_0_), channel_id=1, source_target_pairs={{1,4},{3,5},{5,2},{7,3},{9,12},{11,13},{13,10},{15,11},{17,20},{19... | collective-permute-start | bytes 786440 | tf_op jit(solution)/shard_map/ppermute | solution.py:280
  27.9 10.4 %collective-permute-start.6 = (bf16[4,128,256]{2,1,0:T(8,128)(2,1)S(1)}, bf16[4,128,256]{2,1,0:T(8,128)(2,1)S(1)}, u32[]{:S(2)}, u32[]{:S(2)}) collective-permute-start(bf16[4,128,256]{2,1,0:T(8,128)(2,1)S(1)} %regroup.1.refs_0_), channel_id=1, source_target_pairs={{0,4},{2,5},{4,2},{6,3},{8,12},{10,13},{12,10},{14,11},{16,20},{18... | collective-permute-start | bytes 786440 | tf_op jit(solution)/shard_map/ppermute | solution.py:280
  29.2 9.1 %collective-permute-start.3 = (bf16[4,128,256]{2,1,0:T(8,128)(2,1)S(1)}, bf16[4,128,256]{2,1,0:T(8,128)(2,1)S(1)}, u32[]{:S(2)}, u32[]{:S(2)}) collective-permute-start(bf16[4,128,256]{2,1,0:T(8,128)(2,1)S(1)} %regroup.1.refs_0_), channel_id=1, source_target_pairs={{0,1},{1,0},{2,3},{3,2},{4,5},{5,4},{6,7},{7,6},{8,9},{9,8},{10,11... | collective-permute-start | bytes 786440 | tf_op jit(solution)/shard_map/ppermute | solution.py:287
  34.3 5.2 %collective-permute-start.5 = (bf16[4,128,256]{2,1,0:T(8,128)(2,1)S(1)}, bf16[4,128,256]{2,1,0:T(8,128)(2,1)S(1)}, u32[]{:S(2)}, u32[]{:S(2)}) collective-permute-start(bf16[4,128,256]{2,1,0:T(8,128)(2,1)S(1)} %collective-permute-done.4.refs_2_), channel_id=1, source_target_pairs={{0,1},{1,0},{2,3},{3,2},{4,5},{5,4},{6,7},{7,6},{8,9},{9,8},{10,11... | collective-permute-start | bytes 786440 | tf_op jit(solution)/shard_map/ppermute | solution.py:288

commit v3 on v2

--- a/solution.py
+++ b/solution.py
@@ -166,6 +166,22 @@
     )(gains.reshape(1, inputs), taps, dft_rows(channels), samples)
 
 
+def hold_body(source, out):
+    out[...] = source[...]
+
+
+def hold(array):
+    return pl.pallas_call(
+        hold_body,
+        out_shape=jax.ShapeDtypeStruct(array.shape, array.dtype),
+        in_specs=[pl.BlockSpec(memory_space=pltpu.VMEM)],
+        out_specs=pl.BlockSpec(memory_space=pltpu.VMEM),
+        compiler_params=pltpu.CompilerParams(vmem_limit_bytes=2 * 2**20),
+        cost_estimate=pl.CostEstimate(flops=4 * 10**10, bytes_accessed=0, transcendentals=0),
+        name="hold",
+    )(array)
+
+
 def regroup_body(*refs, half):
     groups = len(refs) - 2
     sources, out, ordered = refs[:groups], refs[groups], refs[groups + 1]
@@ -197,73 +213,87 @@
     )(*sources)
 
 
-def products_body(*refs, half, parts):
-    rows_in = [refs[4 * part : 4 * part + 4] for part in range(parts)]
-    cols_in = [refs[4 * parts + 2 * part : 4 * parts + 2 * part + 2] for part in range(parts)]
-    real, imag, left, right = refs[6 * parts :]
+def products_body(*refs, half):
+    rows_in, cols_in = refs[0:4], refs[4:6]
+    outs, right, staged, sems = refs[6:8], refs[8], refs[9:11], refs[11]
     row, col = lax.axis_index("row"), lax.axis_index("col")
     y, core = col // 2, lax.rem(col, 2)
-    width = rows_in[0][0].shape[2]
-    deep = 4 * half
-    for part in range(parts):
-        down = slice(part * deep, (part + 1) * deep)
+    deep, width = rows_in[0].shape[1:]
+    columns = 2 * width
+    copies = []
+    for k in range(CH_DEV):
         for flip_y in range(2):
-            for flip_core in range(2):
-                block = (y + flip_y) % 2 * 2 + (core + flip_core) % 2
-                left[block, down, :] = rows_in[part][2 * flip_y + flip_core][0]
-    for t in range(2):
-        across = slice(t * width, (t + 1) * width)
-
-        @pl.when(row == y)
-        def _():
-            right[:, across] = left[core * 2 + t]
+
+            @pl.when((row == y) & ((core != y) if flip_y else (core == y)))
+            def _():
+                for flip_core in range(2):
+                    at = pl.multiple_of(lax.rem(core + flip_core, 2) * width, width)
+                    right[k, :, pl.ds(at, width)] = rows_in[2 * flip_y + flip_core][k]
 
         @pl.when(row != y)
         def _():
-            for part in range(parts):
-                down = slice(part * deep, (part + 1) * deep)
-                right[down, across] = cols_in[part][t][0]
-
-    columns = 2 * width
-    for at in range(0, parts * deep, 2 * half):
-        re, im = right[at : at + half, 0:columns], right[at + half : at + 2 * half, 0:columns]
-        right[at : at + half, columns : 2 * columns] = -im
-        right[at + half : at + 2 * half, columns : 2 * columns] = re
-    for block in range(4):
-        product = lax.dot_general(
-            left[block],
-            right[...],
-            (((0,), (0,)), ((), ())),
-            preferred_element_type=jnp.float32,
-        )
-        at = slice(block * width, (block + 1) * width)
-        real[0, at, :] = product[:, 0:columns].astype(jnp.bfloat16)
-        imag[0, at, :] = product[:, columns : 2 * columns].astype(jnp.bfloat16)
+            for t in range(2):
+                right[k, :, t * width : (t + 1) * width] = cols_in[t][k]
+
+        for at in range(0, deep, 2 * half):
+            re = right[k, at : at + half, 0:columns]
+            im = right[k, at + half : at + 2 * half, 0:columns]
+            right[k, at : at + half, columns : 2 * columns] = -im
+            right[k, at + half : at + 2 * half, columns : 2 * columns] = re
+        for begin in range(0, 4, TOGETHER):
+            sources = range(begin, begin + TOGETHER)
+            product = lax.dot_general(
+                jnp.concatenate([rows_in[source][k] for source in sources], axis=1),
+                right[k],
+                (((0,), (0,)), ((), ())),
+                preferred_element_type=jnp.float32,
+            )
+            for source in sources:
+                from_row = (source - begin) * width
+                block = lax.rem(y + source // 2, 2) * 2 + lax.rem(core + source % 2, 2)
+                to = pl.ds(pl.multiple_of(block * width, width), width)
+                for q in range(2):
+                    staged[q][k, source * width : (source + 1) * width, :] = product[
+                        from_row : from_row + width, q * columns : (q + 1) * columns
+                    ].astype(jnp.bfloat16)
+                    copy = pltpu.make_async_copy(
+                        staged[q].at[k, pl.ds(source * width, width), :],
+                        outs[q].at[k, to, :],
+                        sems.at[k, source, q],
+                    )
+                    copy.start()
+                    copies.append(copy)
+    for copy in copies:
+        copy.wait()
 
 
 def products(row_blocks, col_blocks, half):
-    parts = len(row_blocks)
     _, deep, width = row_blocks[0][0].shape
     flat = [a for part in row_blocks for a in part] + [a for part in col_blocks for a in part]
-    out = jax.ShapeDtypeStruct((CH_DEV, 4 * width, 2 * width), jnp.bfloat16)
+    shape = (CH_DEV, 4 * width, 2 * width)
+    out = jax.ShapeDtypeStruct(shape, jnp.bfloat16)
     return pl.pallas_call(
-        functools.partial(products_body, half=half, parts=parts),
-        grid=(CH_DEV,),
-        in_specs=[pl.BlockSpec((1, deep, width), lambda k: (k, 0, 0))] * len(flat),
-        out_specs=[pl.BlockSpec((1, 4 * width, 2 * width), lambda k: (k, 0, 0))] * 2,
+        functools.partial(products_body, half=half),
+        in_specs=[pl.BlockSpec(memory_space=pltpu.VMEM)] * len(flat),
+        out_specs=[pl.BlockSpec(memory_space=pltpu.HBM)] * 2,
         out_shape=[out, out],
         scratch_shapes=[
-            pltpu.VMEM((4, parts * deep, width), jnp.bfloat16),
-            pltpu.VMEM((parts * deep, 4 * width), jnp.bfloat16),
+            pltpu.VMEM((CH_DEV, deep, 4 * width), jnp.bfloat16),
+            pltpu.VMEM(shape, jnp.bfloat16),
+            pltpu.VMEM(shape, jnp.bfloat16),
+            pltpu.SemaphoreType.DMA((CH_DEV, 4, 2)),
         ],
-        compiler_params=pltpu.CompilerParams(vmem_limit_bytes=24 * 2**20),
+        compiler_params=pltpu.CompilerParams(vmem_limit_bytes=28 * 2**20),
         cost_estimate=pl.CostEstimate(
-            flops=2 * CH_DEV * parts * deep * 16 * width * width,
+            flops=2 * CH_DEV * deep * 16 * width * width,
             bytes_accessed=2 * 2 * CH_DEV * 8 * width * width,
             transcendentals=0,
         ),
         name="products",
     )(*flat)
+
+
+TOGETHER = 1
 
 
 def exchange(sent, groups):
@@ -298,7 +328,9 @@
         sent = channelize(
             samples, input_gains, filter_taps, part * 2 * half, half, CUTS, groups
         )
-        mine = regroup(exchange(sent, groups), half)
+        turned = exchange(sent, groups)
+        turned[1] = hold(turned[1])
+        mine = regroup(turned, half)
         rows, columns = gather(mine)
         row_blocks.append(rows)
         col_blocks.append(columns)

time: 44.5 us -> 42.9 us (0.964)
  local copies, waits for them, and re-layouts: 0.84 us -> 0.01 us
  Pallas kernels: 18.7 us -> 17.9 us
    unnamed x2, local copies, waits for them, and re-layouts: 0.84 us -> 0.01 us
    pallas_call x1 -> x2, Pallas kernels: 4.79 us -> 4.03 us  [the longest x1 4.02 us: products(): pl.pallas_call(functools.partial(products_body, half=half), in_specs=[pl....]
where the time goes in v3:
time: 42.9 us; the launch traced here: 42.7 us
  Pallas kernels  17.9 us (42%)
  starting transfers between devices  13.6 us (32%)
  waiting for transfers between devices  10.5 us (24%)
  between operations  0.67 us (2%)
    pallas_call x1, Pallas kernels, channelize(): pl.pallas_call(functools.partial(channelize_body, first=first, half=half,...  13.7 us
    ppermute x3, waiting for transfers between devices, exchange(): lax.ppermute(sent[s], 'freq', moves[s])  4.71 us
    ppermute x1, waiting for transfers between devices, gather(): far_y = lax.ppermute(mine, 'col', other_y)  4.59 us
    ppermute x1, starting transfers between devices, gather(): far = lax.ppermute(far_y, 'col', other_core)  4.07 us
    pallas_call x1, Pallas kernels, products(): pl.pallas_call(functools.partial(products_body, half=half), in_specs=[pl....  4.02 us
    ppermute x2, starting transfers between devices, gather(): lax.ppermute(mine, ('row', 'col'), [(place(x, y, c), place(1 - x, x, y))...  3.97 us
    ppermute x3, starting transfers between devices, exchange(): lax.ppermute(sent[s], 'freq', moves[s])  3.83 us
    ppermute x1, starting transfers between devices, gather(): far_y = lax.ppermute(mine, 'col', other_y)  1.3 us
  transfers between devices with their start and end apart: 8, of which 5 were waited for; matrix products, arithmetic and copies ran while one was open for 0% of the time, Pallas kernels for 0%

profile of v3, /device:TPU:11, one launch (start us, length us, event | category | flops | bytes accessed | tf_op | source)
XLA Modules:
  0.0 42.7 jit_solution(6616357605653273717)
XLA Ops:
  0.6 13.7 %channelize.1 = (bf16[4,64,128]{2,1,0:T(8,128)(2,1)}, bf16[4,64,128]{2,1,0:T(8,128)(2,1)}, bf16[4,64,128]{2,1,0:T(8,128)(2,1)}, bf16[4,64,128]{2,1,0:T(8,128)(2,1)}) custom-call(f32[1,64]{1,0:T(1,128)} %bitcast.1, f32[4,1024]{1,0:T(4,128)} %taps_hbm.1, bf16[32,2048]{1,0:T(8,128)(2,1)} %constant.3.table_hbm, s32[2,64,68608]{2,1,0:T(8,128)} %samples_ref.1), custom_call_target="tpu_custom_call" | custom-call | flops 4496293888 | bytes 35127296 | tf_op jit(solution)/shard_map/channelize/pallas_call | solution.py:140
  14.4 2.4 %collective-permute-start = (bf16[4,64,128]{2,1,0:T(8,128)(2,1)}, bf16[4,64,128]{2,1,0:T(8,128)(2,1)S(1)}, u32[]{:S(2)}, u32[]{:S(2)}) collective-permute-start(bf16[4,64,128]{2,1,0:T(8,128)(2,1)} %get-tuple-element.7), channel_id=1, source_target_pairs={{0,16},{8,24},{16,0},{24,8},{1,17},{9,25},{17,1},{25,9},{2,18},{10... | collective-permute-start | bytes 196616 | tf_op jit(solution)/shard_map/ppermute | solution.py:301
  16.7 0.0 collective-permute-start.1
  16.7 0.0 copy-start
  16.7 1.5 %collective-permute-start.2 = (bf16[4,64,128]{2,1,0:T(8,128)(2,1)}, bf16[4,64,128]{2,1,0:T(8,128)(2,1)S(1)}, u32[]{:S(2)}, u32[]{:S(2)}) collective-permute-start(bf16[4,64,128]{2,1,0:T(8,128)(2,1)} %get-tuple-element.9), channel_id=1, source_target_pairs={{0,24},{8,0},{16,8},{24,16},{1,25},{9,1},{17,9},{25,17},{2,26},{10... | collective-permute-start | bytes 196616 | tf_op jit(solution)/shard_map/ppermute | solution.py:301
  18.2 1.1 %collective-permute-done.source = bf16[4,64,128]{2,1,0:T(8,128)(2,1)S(1)} collective-permute-done((bf16[4,64,128]{2,1,0:T(8,128)(2,1)}, bf16[4,64,128]{2,1,0:T(8,128)(2,1)S(1)}, u32[]{:S(2)}, u32[]{:S(2)}) %collective-permute-start) | collective-permute-done | bytes 65568 | tf_op jit(solution)/shard_map/ppermute | solution.py:301
  19.3 2.0 %collective-permute-done.1.refs_2_ = bf16[4,64,128]{2,1,0:T(8,128)(2,1)S(1)} collective-permute-done((bf16[4,64,128]{2,1,0:T(8,128)(2,1)}, bf16[4,64,128]{2,1,0:T(8,128)(2,1)S(1)}, u32[]{:S(2)}, u32[]{:S(2)}) %collective-permute-start.1) | collective-permute-done | bytes 65568 | tf_op jit(solution)/shard_map/ppermute | solution.py:301
  21.3 1.6 %collective-permute-done.2.refs_3_ = bf16[4,64,128]{2,1,0:T(8,128)(2,1)S(1)} collective-permute-done((bf16[4,64,128]{2,1,0:T(8,128)(2,1)}, bf16[4,64,128]{2,1,0:T(8,128)(2,1)S(1)}, u32[]{:S(2)}, u32[]{:S(2)}) %collective-permute-start.2) | collective-permute-done | bytes 65568 | tf_op jit(solution)/shard_map/ppermute | solution.py:301
  22.9 0.0 copy-done
  22.9 0.2 regroup.1.refs_0_
  23.1 1.3 %collective-permute-start.4 = (bf16[4,128,256]{2,1,0:T(8,128)(2,1)S(1)}, bf16[4,128,256]{2,1,0:T(8,128)(2,1)S(1)}, u32[]{:S(2)}, u32[]{:S(2)}) collective-permute-start(bf16[4,128,256]{2,1,0:T(8,128)(2,1)S(1)} %regroup.1.refs_0_), channel_id=1, source_target_pairs={{0,2},{2,0},{1,3},{3,1},{4,6},{6,4},{5,7},{7,5},{8,10},{10,8},{9,1... | collective-permute-start | bytes 786440 | tf_op jit(solution)/shard_map/ppermute | solution.py:308
  24.4 2.7 %collective-permute-start.7 = (bf16[4,128,256]{2,1,0:T(8,128)(2,1)S(1)}, bf16[4,128,256]{2,1,0:T(8,128)(2,1)S(1)}, u32[]{:S(2)}, u32[]{:S(2)}) collective-permute-start(bf16[4,128,256]{2,1,0:T(8,128)(2,1)S(1)} %regroup.1.refs_0_), channel_id=1, source_target_pairs={{1,4},{3,5},{5,2},{7,3},{9,12},{11,13},{13,10},{15,11},{17,20},{19... | collective-permute-start | bytes 786440 | tf_op jit(solution)/shard_map/ppermute | solution.py:310
  27.1 1.3 %collective-permute-start.6 = (bf16[4,128,256]{2,1,0:T(8,128)(2,1)S(1)}, bf16[4,128,256]{2,1,0:T(8,128)(2,1)S(1)}, u32[]{:S(2)}, u32[]{:S(2)}) collective-permute-start(bf16[4,128,256]{2,1,0:T(8,128)(2,1)S(1)} %regroup.1.refs_0_), channel_id=1, source_target_pairs={{0,4},{2,5},{4,2},{6,3},{8,12},{10,13},{12,10},{14,11},{16,20},{18... | collective-permute-start | bytes 786440 | tf_op jit(solution)/shard_map/ppermute | solution.py:310
  28.4 0.5 %collective-permute-start.3 = (bf16[4,128,256]{2,1,0:T(8,128)(2,1)S(1)}, bf16[4,128,256]{2,1,0:T(8,128)(2,1)S(1)}, u32[]{:S(2)}, u32[]{:S(2)}) collective-permute-start(bf16[4,128,256]{2,1,0:T(8,128)(2,1)S(1)} %regroup.1.refs_0_), channel_id=1, source_target_pairs={{0,1},{1,0},{2,3},{3,2},{4,5},{5,4},{6,7},{7,6},{8,9},{9,8},{10,11... | collective-permute-start | bytes 786440 | tf_op jit(solution)/shard_map/ppermute | solution.py:317
  28.8 4.6 %collective-permute-done.4.refs_2_ = bf16[4,128,256]{2,1,0:T(8,128)(2,1)S(1)} collective-permute-done((bf16[4,128,256]{2,1,0:T(8,128)(2,1)S(1)}, bf16[4,128,256]{2,1,0:T(8,128)(2,1)S(1)}, u32[]{:S(2)}, u32[]{:S(2)}) %collective-permute-start.4) | collective-permute-done | bytes 262176 | tf_op jit(solution)/shard_map/ppermute | solution.py:308
  33.4 4.1 %collective-permute-start.5 = (bf16[4,128,256]{2,1,0:T(8,128)(2,1)S(1)}, bf16[4,128,256]{2,1,0:T(8,128)(2,1)S(1)}, u32[]{:S(2)}, u32[]{:S(2)}) collective-permute-start(bf16[4,128,256]{2,1,0:T(8,128)(2,1)S(1)} %collective-permute-done.4.refs_2_), channel_id=1, source_target_pairs={{0,1},{1,0},{2,3},{3,2},{4,5},{5,4},{6,7},{7,6},{8,9},{9,8},{10,11... | collective-permute-start | bytes 786440 | tf_op jit(solution)/shard_map/ppermute | solution.py:318
  37.5 0.0 collective-permute-done.7.refs_5_
  37.5 0.0 collective-permute-done.6.refs_4_
  37.5 0.0 collective-permute-done.3.refs_1_
  37.5 1.1 %collective-permute-done.5.refs_3_ = bf16[4,128,256]{2,1,0:T(8,128)(2,1)S(1)} collective-permute-done((bf16[4,128,256]{2,1,0:T(8,128)(2,1)S(1)}, bf16[4,128,256]{2,1,0:T(8,128)(2,1)S(1)}, u32[]{:S(2)}, u32[]{:S(2)}) %collective-permute-start.5) | collective-permute-done | bytes 262176 | tf_op jit(solution)/shard_map/ppermute | solution.py:318
  38.7 4.0 %products.1 = (bf16[4,1024,512]{2,1,0:T(8,128)(2,1)}, bf16[4,1024,512]{2,1,0:T(8,128)(2,1)}) custom-call(bf16[4,128,256]{2,1,0:T(8,128)(2,1)S(1)} %regroup.1.refs_0_, bf16[4,128,256]{2,1,0:T(8,128)(2,1)S(1)} %collective-permute-done.3.refs_1_, bf16[4,128,256]{2,1,0:T(8,128)(2,1)S(1)} %collective-permute-done.4.refs_2_, ...), custom_call_target="tpu_custom_call" | custom-call | flops 1073741824 | bytes 8388608 | tf_op jit(solution)/shard_map/products/pallas_call | solution.py:275
  (1 shorter events, 0.0 us)
Async XLA Ops:
  14.4 4.9 %collective-permute-start = (bf16[4,64,128]{2,1,0:T(8,128)(2,1)}, bf16[4,64,128]{2,1,0:T(8,128)(2,1)S(1)}, u32[]{:S(2)}, u32[]{:S(2)}) collective-permute-start(bf16[4,64,128]{2,1,0:T(8,128)(2,1)} %get-tuple-element.7), channel_id=1, source_target_pairs={{0,16},{8,24},{16,0},{24,8},{1,17},{9,25},{17,1},{25,9},{2,18},{10... | collective-permute-start | bytes 196616 | tf_op jit(solution)/shard_map/ppermute | solution.py:301
  16.7 4.6 %collective-permute-start.1 = (bf16[4,64,128]{2,1,0:T(8,128)(2,1)}, bf16[4,64,128]{2,1,0:T(8,128)(2,1)S(1)}, u32[]{:S(2)}, u32[]{:S(2)}) collective-permute-start(bf16[4,64,128]{2,1,0:T(8,128)(2,1)} %get-tuple-element.8), channel_id=1, source_target_pairs={{0,8},{8,16},{16,24},{24,0},{1,9},{9,17},{17,25},{25,1},{2,10},{10... | collective-permute-start | bytes 196616 | tf_op jit(solution)/shard_map/ppermute | solution.py:301
  16.7 6.2 %copy-start = (bf16[4,64,128]{2,1,0:T(8,128)(2,1)S(1)}, bf16[4,64,128]{2,1,0:T(8,128)(2,1)}, u32[]{:S(2)}) copy-start(bf16[4,64,128]{2,1,0:T(8,128)(2,1)} %get-tuple-element.6.refs_0_) | copy-start | bytes 196612
  16.7 6.2 %collective-permute-start.2 = (bf16[4,64,128]{2,1,0:T(8,128)(2,1)}, bf16[4,64,128]{2,1,0:T(8,128)(2,1)S(1)}, u32[]{:S(2)}, u32[]{:S(2)}) collective-permute-start(bf16[4,64,128]{2,1,0:T(8,128)(2,1)} %get-tuple-element.9), channel_id=1, source_target_pairs={{0,24},{8,0},{16,8},{24,16},{1,25},{9,1},{17,9},{25,17},{2,26},{10... | collective-permute-start | bytes 196616 | tf_op jit(solution)/shard_map/ppermute | solution.py:301
  23.1 10.3 %collective-permute-start.4 = (bf16[4,128,256]{2,1,0:T(8,128)(2,1)S(1)}, bf16[4,128,256]{2,1,0:T(8,128)(2,1)S(1)}, u32[]{:S(2)}, u32[]{:S(2)}) collective-permute-start(bf16[4,128,256]{2,1,0:T(8,128)(2,1)S(1)} %regroup.1.refs_0_), channel_id=1, source_target_pairs={{0,2},{2,0},{1,3},{3,1},{4,6},{6,4},{5,7},{7,5},{8,10},{10,8},{9,1... | collective-permute-start | bytes 786440 | tf_op jit(solution)/shard_map/ppermute | solution.py:308
  24.4 13.1 %collective-permute-start.7 = (bf16[4,128,256]{2,1,0:T(8,128)(2,1)S(1)}, bf16[4,128,256]{2,1,0:T(8,128)(2,1)S(1)}, u32[]{:S(2)}, u32[]{:S(2)}) collective-permute-start(bf16[4,128,256]{2,1,0:T(8,128)(2,1)S(1)} %regroup.1.refs_0_), channel_id=1, source_target_pairs={{1,4},{3,5},{5,2},{7,3},{9,12},{11,13},{13,10},{15,11},{17,20},{19... | collective-permute-start | bytes 786440 | tf_op jit(solution)/shard_map/ppermute | solution.py:310
  27.1 10.4 %collective-permute-start.6 = (bf16[4,128,256]{2,1,0:T(8,128)(2,1)S(1)}, bf16[4,128,256]{2,1,0:T(8,128)(2,1)S(1)}, u32[]{:S(2)}, u32[]{:S(2)}) collective-permute-start(bf16[4,128,256]{2,1,0:T(8,128)(2,1)S(1)} %regroup.1.refs_0_), channel_id=1, source_target_pairs={{0,4},{2,5},{4,2},{6,3},{8,12},{10,13},{12,10},{14,11},{16,20},{18... | collective-permute-start | bytes 786440 | tf_op jit(solution)/shard_map/ppermute | solution.py:310
  28.4 9.1 %collective-permute-start.3 = (bf16[4,128,256]{2,1,0:T(8,128)(2,1)S(1)}, bf16[4,128,256]{2,1,0:T(8,128)(2,1)S(1)}, u32[]{:S(2)}, u32[]{:S(2)}) collective-permute-start(bf16[4,128,256]{2,1,0:T(8,128)(2,1)S(1)} %regroup.1.refs_0_), channel_id=1, source_target_pairs={{0,1},{1,0},{2,3},{3,2},{4,5},{5,4},{6,7},{7,6},{8,9},{9,8},{10,11... | collective-permute-start | bytes 786440 | tf_op jit(solution)/shard_map/ppermute | solution.py:317
  33.4 5.2 %collective-permute-start.5 = (bf16[4,128,256]{2,1,0:T(8,128)(2,1)S(1)}, bf16[4,128,256]{2,1,0:T(8,128)(2,1)S(1)}, u32[]{:S(2)}, u32[]{:S(2)}) collective-permute-start(bf16[4,128,256]{2,1,0:T(8,128)(2,1)S(1)} %collective-permute-done.4.refs_2_), channel_id=1, source_target_pairs={{0,1},{1,0},{2,3},{3,2},{4,5},{5,4},{6,7},{7,6},{8,9},{9,8},{10,11... | collective-permute-start | bytes 786440 | tf_op jit(solution)/shard_map/ppermute | solution.py:318

commit v4 on v3

--- a/solution.py
+++ b/solution.py
@@ -14,7 +14,7 @@
 SPEC = 64
 CH_DEV = 4
 LANES = 128
-AHEAD = 3
+AHEAD = 2
 VMEM_BYTES = 60 * 2**20
 
 
@@ -46,7 +46,8 @@
     gain_hbm, taps_hbm, table_hbm, samples_ref, *rest, first, half, blocks, groups
 ):
     outs, scratch = rest[:groups], rest[groups:]
-    gain_ref, taps_ref, table_ref, weights, raw, lhs, sums, held, sems, small_sems = scratch
+    gain_ref, taps_ref, table_ref, weights, raw, lhs, sums, held, staged = scratch[:9]
+    sems, small_sems, out_sems = scratch[9:]
     inputs = samples_ref.shape[1]
     rows = table_ref.shape[0]
     small = [
@@ -73,6 +74,9 @@
             copy.start()
     for copy in small:
         copy.wait()
+    for index in range(AHEAD, len(blocks)):
+        for copy in copies[index]:
+            copy.start()
     for p in range(2):
         for b in range(NFFT // LANES):
             table = table_ref[:, p * NFFT + b * LANES : p * NFFT + (b + 1) * LANES].astype(
@@ -90,9 +94,6 @@
     for index, (start, stop) in enumerate(blocks):
         for copy in copies[index]:
             copy.wait()
-        if index + AHEAD < len(blocks):
-            for copy in copies[index + AHEAD]:
-                copy.start()
         buffer = lhs[index % 2]
         for slot in range(start, stop):
             for side in range(2):
@@ -121,12 +122,17 @@
             held[pl.ds(slot, rows, stride=half), :] = total * gain
     me = lax.axis_index("freq")
     depth = 2 * half
+    sent = []
     for s in range(groups):
         to = partner(me, s, groups) * (CH_DEV * depth)
         for k in range(CH_DEV):
-            outs[s][k] = held[
+            staged[s, k] = held[
                 pl.ds(pl.multiple_of(to + k * depth, 8), depth), :
             ].astype(jnp.bfloat16)
+        sent.append(pltpu.make_async_copy(staged.at[s], outs[s], out_sems.at[s]))
+        sent[-1].start()
+    for copy in sent:
+        copy.wait()
 
 
 def channelize(samples, gains, taps, first, half, cuts, groups):
@@ -142,7 +148,7 @@
             channelize_body, first=first, half=half, blocks=blocks, groups=groups
         ),
         in_specs=[pl.BlockSpec(memory_space=pltpu.HBM)] * 4,
-        out_specs=[pl.BlockSpec(memory_space=pltpu.VMEM)] * groups,
+        out_specs=[pl.BlockSpec(memory_space=pltpu.HBM)] * groups,
         out_shape=[jax.ShapeDtypeStruct((CH_DEV, 2 * half, LANES), jnp.bfloat16)] * groups,
         scratch_shapes=[
             pltpu.VMEM((1, inputs), jnp.float32),
@@ -153,8 +159,10 @@
             [pltpu.VMEM((widest * 2 * inputs, 2 * NFFT), jnp.bfloat16)] * 2,
             pltpu.VMEM((TAPS * rows, slots * LANES), jnp.float32),
             pltpu.VMEM((rows * half, LANES), jnp.float32),
+            pltpu.VMEM((groups, CH_DEV, 2 * half, LANES), jnp.bfloat16),
             pltpu.SemaphoreType.DMA((len(blocks), 2)),
             pltpu.SemaphoreType.DMA((3,)),
+            pltpu.SemaphoreType.DMA((groups,)),
         ],
         compiler_params=pltpu.CompilerParams(vmem_limit_bytes=VMEM_BYTES),
         cost_estimate=pl.CostEstimate(
@@ -338,7 +346,7 @@
 
 
 PARTS = 1
-CUTS = (0, 4, 8, 12, 16, 20, 24, 28, 32, 35)
+CUTS = (0, 3, 7, 11, 15, 19, 23, 27, 31, 35)
 
 
 def dft_table(channels):

time: 42.9 us -> 42.3 us (0.986)
  Pallas kernels: 17.9 us -> 17.4 us
    pallas_call x1, Pallas kernels: 13.7 us -> 13.2 us  [channelize(): pl.pallas_call(functools.partial(channelize_body, first=first, half=half,...]
where the time goes in v4:
time: 42.3 us; the launch traced here: 42.1 us
  Pallas kernels  17.4 us (41%)
  starting transfers between devices  13.7 us (32%)
  waiting for transfers between devices  10.4 us (25%)
  between operations  0.67 us (2%)
    pallas_call x1, Pallas kernels, channelize(): pl.pallas_call(functools.partial(channelize_body, first=first, half=half,...  13.2 us
    ppermute x3, waiting for transfers between devices, exchange(): lax.ppermute(sent[s], 'freq', moves[s])  4.71 us
    ppermute x1, waiting for transfers between devices, gather(): far_y = lax.ppermute(mine, 'col', other_y)  4.54 us
    ppermute x1, starting transfers between devices, gather(): far = lax.ppermute(far_y, 'col', other_core)  4.11 us
    pallas_call x1, Pallas kernels, products(): pl.pallas_call(functools.partial(products_body, half=half), in_specs=[pl....  4.02 us
    ppermute x2, starting transfers between devices, gather(): lax.ppermute(mine, ('row', 'col'), [(place(x, y, c), place(1 - x, x, y))...  3.98 us
    ppermute x3, starting transfers between devices, exchange(): lax.ppermute(sent[s], 'freq', moves[s])  3.84 us
    ppermute x1, starting transfers between devices, gather(): far_y = lax.ppermute(mine, 'col', other_y)  1.3 us
  transfers between devices with their start and end apart: 8, of which 5 were waited for; matrix products, arithmetic and copies ran while one was open for 0% of the time, Pallas kernels for 0%

profile of v4, /device:TPU:11, one launch (start us, length us, event | category | flops | bytes accessed | tf_op | source)
XLA Modules:
  0.0 42.1 jit_solution(7210199375315645370)
XLA Ops:
  0.6 13.2 %channelize.1 = (bf16[4,64,128]{2,1,0:T(8,128)(2,1)}, bf16[4,64,128]{2,1,0:T(8,128)(2,1)}, bf16[4,64,128]{2,1,0:T(8,128)(2,1)}, bf16[4,64,128]{2,1,0:T(8,128)(2,1)}) custom-call(f32[1,64]{1,0:T(1,128)} %bitcast.1, f32[4,1024]{1,0:T(4,128)} %taps_hbm.1, bf16[32,2048]{1,0:T(8,128)(2,1)} %constant.3.table_hbm, s32[2,64,68608]{2,1,0:T(8,128)} %samples_ref.1), custom_call_target="tpu_custom_call" | custom-call | flops 4496293888 | bytes 35127296 | tf_op jit(solution)/shard_map/channelize/pallas_call | solution.py:146
  13.8 2.4 %collective-permute-start = (bf16[4,64,128]{2,1,0:T(8,128)(2,1)}, bf16[4,64,128]{2,1,0:T(8,128)(2,1)S(1)}, u32[]{:S(2)}, u32[]{:S(2)}) collective-permute-start(bf16[4,64,128]{2,1,0:T(8,128)(2,1)} %get-tuple-element.7), channel_id=1, source_target_pairs={{0,16},{8,24},{16,0},{24,8},{1,17},{9,25},{17,1},{25,9},{2,18},{10... | collective-permute-start | bytes 196616 | tf_op jit(solution)/shard_map/ppermute | solution.py:309
  16.2 0.0 collective-permute-start.1
  16.2 0.0 copy-start
  16.2 1.5 %collective-permute-start.2 = (bf16[4,64,128]{2,1,0:T(8,128)(2,1)}, bf16[4,64,128]{2,1,0:T(8,128)(2,1)S(1)}, u32[]{:S(2)}, u32[]{:S(2)}) collective-permute-start(bf16[4,64,128]{2,1,0:T(8,128)(2,1)} %get-tuple-element.9), channel_id=1, source_target_pairs={{0,24},{8,0},{16,8},{24,16},{1,25},{9,1},{17,9},{25,17},{2,26},{10... | collective-permute-start | bytes 196616 | tf_op jit(solution)/shard_map/ppermute | solution.py:309
  17.7 1.1 %collective-permute-done.source = bf16[4,64,128]{2,1,0:T(8,128)(2,1)S(1)} collective-permute-done((bf16[4,64,128]{2,1,0:T(8,128)(2,1)}, bf16[4,64,128]{2,1,0:T(8,128)(2,1)S(1)}, u32[]{:S(2)}, u32[]{:S(2)}) %collective-permute-start) | collective-permute-done | bytes 65568 | tf_op jit(solution)/shard_map/ppermute | solution.py:309
  18.8 2.1 %collective-permute-done.1.refs_2_ = bf16[4,64,128]{2,1,0:T(8,128)(2,1)S(1)} collective-permute-done((bf16[4,64,128]{2,1,0:T(8,128)(2,1)}, bf16[4,64,128]{2,1,0:T(8,128)(2,1)S(1)}, u32[]{:S(2)}, u32[]{:S(2)}) %collective-permute-start.1) | collective-permute-done | bytes 65568 | tf_op jit(solution)/shard_map/ppermute | solution.py:309
  20.8 1.6 %collective-permute-done.2.refs_3_ = bf16[4,64,128]{2,1,0:T(8,128)(2,1)S(1)} collective-permute-done((bf16[4,64,128]{2,1,0:T(8,128)(2,1)}, bf16[4,64,128]{2,1,0:T(8,128)(2,1)S(1)}, u32[]{:S(2)}, u32[]{:S(2)}) %collective-permute-start.2) | collective-permute-done | bytes 65568 | tf_op jit(solution)/shard_map/ppermute | solution.py:309
  22.4 0.0 copy-done
  22.4 0.2 regroup.1.refs_0_
  22.6 1.3 %collective-permute-start.4 = (bf16[4,128,256]{2,1,0:T(8,128)(2,1)S(1)}, bf16[4,128,256]{2,1,0:T(8,128)(2,1)S(1)}, u32[]{:S(2)}, u32[]{:S(2)}) collective-permute-start(bf16[4,128,256]{2,1,0:T(8,128)(2,1)S(1)} %regroup.1.refs_0_), channel_id=1, source_target_pairs={{0,2},{2,0},{1,3},{3,1},{4,6},{6,4},{5,7},{7,5},{8,10},{10,8},{9,1... | collective-permute-start | bytes 786440 | tf_op jit(solution)/shard_map/ppermute | solution.py:316
  23.9 2.7 %collective-permute-start.7 = (bf16[4,128,256]{2,1,0:T(8,128)(2,1)S(1)}, bf16[4,128,256]{2,1,0:T(8,128)(2,1)S(1)}, u32[]{:S(2)}, u32[]{:S(2)}) collective-permute-start(bf16[4,128,256]{2,1,0:T(8,128)(2,1)S(1)} %regroup.1.refs_0_), channel_id=1, source_target_pairs={{1,4},{3,5},{5,2},{7,3},{9,12},{11,13},{13,10},{15,11},{17,20},{19... | collective-permute-start | bytes 786440 | tf_op jit(solution)/shard_map/ppermute | solution.py:318
  26.5 1.3 %collective-permute-start.6 = (bf16[4,128,256]{2,1,0:T(8,128)(2,1)S(1)}, bf16[4,128,256]{2,1,0:T(8,128)(2,1)S(1)}, u32[]{:S(2)}, u32[]{:S(2)}) collective-permute-start(bf16[4,128,256]{2,1,0:T(8,128)(2,1)S(1)} %regroup.1.refs_0_), channel_id=1, source_target_pairs={{0,4},{2,5},{4,2},{6,3},{8,12},{10,13},{12,10},{14,11},{16,20},{18... | collective-permute-start | bytes 786440 | tf_op jit(solution)/shard_map/ppermute | solution.py:318
  27.8 0.5 %collective-permute-start.3 = (bf16[4,128,256]{2,1,0:T(8,128)(2,1)S(1)}, bf16[4,128,256]{2,1,0:T(8,128)(2,1)S(1)}, u32[]{:S(2)}, u32[]{:S(2)}) collective-permute-start(bf16[4,128,256]{2,1,0:T(8,128)(2,1)S(1)} %regroup.1.refs_0_), channel_id=1, source_target_pairs={{0,1},{1,0},{2,3},{3,2},{4,5},{5,4},{6,7},{7,6},{8,9},{9,8},{10,11... | collective-permute-start | bytes 786440 | tf_op jit(solution)/shard_map/ppermute | solution.py:325
  28.3 4.5 %collective-permute-done.4.refs_2_ = bf16[4,128,256]{2,1,0:T(8,128)(2,1)S(1)} collective-permute-done((bf16[4,128,256]{2,1,0:T(8,128)(2,1)S(1)}, bf16[4,128,256]{2,1,0:T(8,128)(2,1)S(1)}, u32[]{:S(2)}, u32[]{:S(2)}) %collective-permute-start.4) | collective-permute-done | bytes 262176 | tf_op jit(solution)/shard_map/ppermute | solution.py:316
  32.8 4.1 %collective-permute-start.5 = (bf16[4,128,256]{2,1,0:T(8,128)(2,1)S(1)}, bf16[4,128,256]{2,1,0:T(8,128)(2,1)S(1)}, u32[]{:S(2)}, u32[]{:S(2)}) collective-permute-start(bf16[4,128,256]{2,1,0:T(8,128)(2,1)S(1)} %collective-permute-done.4.refs_2_), channel_id=1, source_target_pairs={{0,1},{1,0},{2,3},{3,2},{4,5},{5,4},{6,7},{7,6},{8,9},{9,8},{10,11... | collective-permute-start | bytes 786440 | tf_op jit(solution)/shard_map/ppermute | solution.py:326
  37.0 0.0 collective-permute-done.7.refs_5_
  37.0 0.0 collective-permute-done.6.refs_4_
  37.0 0.0 collective-permute-done.3.refs_1_
  37.0 1.1 %collective-permute-done.5.refs_3_ = bf16[4,128,256]{2,1,0:T(8,128)(2,1)S(1)} collective-permute-done((bf16[4,128,256]{2,1,0:T(8,128)(2,1)S(1)}, bf16[4,128,256]{2,1,0:T(8,128)(2,1)S(1)}, u32[]{:S(2)}, u32[]{:S(2)}) %collective-permute-start.5) | collective-permute-done | bytes 262176 | tf_op jit(solution)/shard_map/ppermute | solution.py:326
  38.1 4.0 %products.1 = (bf16[4,1024,512]{2,1,0:T(8,128)(2,1)}, bf16[4,1024,512]{2,1,0:T(8,128)(2,1)}) custom-call(bf16[4,128,256]{2,1,0:T(8,128)(2,1)S(1)} %regroup.1.refs_0_, bf16[4,128,256]{2,1,0:T(8,128)(2,1)S(1)} %collective-permute-done.3.refs_1_, bf16[4,128,256]{2,1,0:T(8,128)(2,1)S(1)} %collective-permute-done.4.refs_2_, ...), custom_call_target="tpu_custom_call" | custom-call | flops 1073741824 | bytes 8388608 | tf_op jit(solution)/shard_map/products/pallas_call | solution.py:283
  (1 shorter events, 0.0 us)
Async XLA Ops:
  13.8 4.9 %collective-permute-start = (bf16[4,64,128]{2,1,0:T(8,128)(2,1)}, bf16[4,64,128]{2,1,0:T(8,128)(2,1)S(1)}, u32[]{:S(2)}, u32[]{:S(2)}) collective-permute-start(bf16[4,64,128]{2,1,0:T(8,128)(2,1)} %get-tuple-element.7), channel_id=1, source_target_pairs={{0,16},{8,24},{16,0},{24,8},{1,17},{9,25},{17,1},{25,9},{2,18},{10... | collective-permute-start | bytes 196616 | tf_op jit(solution)/shard_map/ppermute | solution.py:309
  16.2 4.6 %collective-permute-start.1 = (bf16[4,64,128]{2,1,0:T(8,128)(2,1)}, bf16[4,64,128]{2,1,0:T(8,128)(2,1)S(1)}, u32[]{:S(2)}, u32[]{:S(2)}) collective-permute-start(bf16[4,64,128]{2,1,0:T(8,128)(2,1)} %get-tuple-element.8), channel_id=1, source_target_pairs={{0,8},{8,16},{16,24},{24,0},{1,9},{9,17},{17,25},{25,1},{2,10},{10... | collective-permute-start | bytes 196616 | tf_op jit(solution)/shard_map/ppermute | solution.py:309
  16.2 6.2 %copy-start = (bf16[4,64,128]{2,1,0:T(8,128)(2,1)S(1)}, bf16[4,64,128]{2,1,0:T(8,128)(2,1)}, u32[]{:S(2)}) copy-start(bf16[4,64,128]{2,1,0:T(8,128)(2,1)} %get-tuple-element.6.refs_0_) | copy-start | bytes 196612
  16.2 6.2 %collective-permute-start.2 = (bf16[4,64,128]{2,1,0:T(8,128)(2,1)}, bf16[4,64,128]{2,1,0:T(8,128)(2,1)S(1)}, u32[]{:S(2)}, u32[]{:S(2)}) collective-permute-start(bf16[4,64,128]{2,1,0:T(8,128)(2,1)} %get-tuple-element.9), channel_id=1, source_target_pairs={{0,24},{8,0},{16,8},{24,16},{1,25},{9,1},{17,9},{25,17},{2,26},{10... | collective-permute-start | bytes 196616 | tf_op jit(solution)/shard_map/ppermute | solution.py:309
  22.6 10.3 %collective-permute-start.4 = (bf16[4,128,256]{2,1,0:T(8,128)(2,1)S(1)}, bf16[4,128,256]{2,1,0:T(8,128)(2,1)S(1)}, u32[]{:S(2)}, u32[]{:S(2)}) collective-permute-start(bf16[4,128,256]{2,1,0:T(8,128)(2,1)S(1)} %regroup.1.refs_0_), channel_id=1, source_target_pairs={{0,2},{2,0},{1,3},{3,1},{4,6},{6,4},{5,7},{7,5},{8,10},{10,8},{9,1... | collective-permute-start | bytes 786440 | tf_op jit(solution)/shard_map/ppermute | solution.py:316
  23.9 13.1 %collective-permute-start.7 = (bf16[4,128,256]{2,1,0:T(8,128)(2,1)S(1)}, bf16[4,128,256]{2,1,0:T(8,128)(2,1)S(1)}, u32[]{:S(2)}, u32[]{:S(2)}) collective-permute-start(bf16[4,128,256]{2,1,0:T(8,128)(2,1)S(1)} %regroup.1.refs_0_), channel_id=1, source_target_pairs={{1,4},{3,5},{5,2},{7,3},{9,12},{11,13},{13,10},{15,11},{17,20},{19... | collective-permute-start | bytes 786440 | tf_op jit(solution)/shard_map/ppermute | solution.py:318
  26.5 10.4 %collective-permute-start.6 = (bf16[4,128,256]{2,1,0:T(8,128)(2,1)S(1)}, bf16[4,128,256]{2,1,0:T(8,128)(2,1)S(1)}, u32[]{:S(2)}, u32[]{:S(2)}) collective-permute-start(bf16[4,128,256]{2,1,0:T(8,128)(2,1)S(1)} %regroup.1.refs_0_), channel_id=1, source_target_pairs={{0,4},{2,5},{4,2},{6,3},{8,12},{10,13},{12,10},{14,11},{16,20},{18... | collective-permute-start | bytes 786440 | tf_op jit(solution)/shard_map/ppermute | solution.py:318
  27.8 9.1 %collective-permute-start.3 = (bf16[4,128,256]{2,1,0:T(8,128)(2,1)S(1)}, bf16[4,128,256]{2,1,0:T(8,128)(2,1)S(1)}, u32[]{:S(2)}, u32[]{:S(2)}) collective-permute-start(bf16[4,128,256]{2,1,0:T(8,128)(2,1)S(1)} %regroup.1.refs_0_), channel_id=1, source_target_pairs={{0,1},{1,0},{2,3},{3,2},{4,5},{5,4},{6,7},{7,6},{8,9},{9,8},{10,11... | collective-permute-start | bytes 786440 | tf_op jit(solution)/shard_map/ppermute | solution.py:325
  32.8 5.3 %collective-permute-start.5 = (bf16[4,128,256]{2,1,0:T(8,128)(2,1)S(1)}, bf16[4,128,256]{2,1,0:T(8,128)(2,1)S(1)}, u32[]{:S(2)}, u32[]{:S(2)}) collective-permute-start(bf16[4,128,256]{2,1,0:T(8,128)(2,1)S(1)} %collective-permute-done.4.refs_2_), channel_id=1, source_target_pairs={{0,1},{1,0},{2,3},{3,2},{4,5},{5,4},{6,7},{7,6},{8,9},{9,8},{10,11... | collective-permute-start | bytes 786440 | tf_op jit(solution)/shard_map/ppermute | solution.py:326

commit v5 on v4

--- a/solution.py
+++ b/solution.py
@@ -15,6 +15,7 @@
 CH_DEV = 4
 LANES = 128
 AHEAD = 2
+PAD = 16
 VMEM_BYTES = 60 * 2**20
 
 
@@ -125,11 +126,14 @@
     sent = []
     for s in range(groups):
         to = partner(me, s, groups) * (CH_DEV * depth)
-        for k in range(CH_DEV):
-            staged[s, k] = held[
-                pl.ds(pl.multiple_of(to + k * depth, 8), depth), :
-            ].astype(jnp.bfloat16)
-        sent.append(pltpu.make_async_copy(staged.at[s], outs[s], out_sems.at[s]))
+        size = CH_DEV * depth
+        staged[s, 0:size] = held[pl.ds(pl.multiple_of(to, 8), size), :].astype(jnp.bfloat16)
+        if s:
+            staged[s, size : size + PAD] = jnp.zeros((PAD, LANES), jnp.bfloat16)
+            size += PAD
+        sent.append(
+            pltpu.make_async_copy(staged.at[s, pl.ds(0, size), :], outs[s], out_sems.at[s])
+        )
         sent[-1].start()
     for copy in sent:
         copy.wait()
@@ -149,7 +153,10 @@
         ),
         in_specs=[pl.BlockSpec(memory_space=pltpu.HBM)] * 4,
         out_specs=[pl.BlockSpec(memory_space=pltpu.HBM)] * groups,
-        out_shape=[jax.ShapeDtypeStruct((CH_DEV, 2 * half, LANES), jnp.bfloat16)] * groups,
+        out_shape=[
+            jax.ShapeDtypeStruct((CH_DEV * 2 * half + (PAD if s else 0), LANES), jnp.bfloat16)
+            for s in range(groups)
+        ],
         scratch_shapes=[
             pltpu.VMEM((1, inputs), jnp.float32),
             pltpu.VMEM((TAPS, NFFT), jnp.float32),
@@ -159,7 +166,7 @@
             [pltpu.VMEM((widest * 2 * inputs, 2 * NFFT), jnp.bfloat16)] * 2,
             pltpu.VMEM((TAPS * rows, slots * LANES), jnp.float32),
             pltpu.VMEM((rows * half, LANES), jnp.float32),
-            pltpu.VMEM((groups, CH_DEV, 2 * half, LANES), jnp.bfloat16),
+            pltpu.VMEM((groups, CH_DEV * 2 * half + PAD, LANES), jnp.bfloat16),
             pltpu.SemaphoreType.DMA((len(blocks), 2)),
             pltpu.SemaphoreType.DMA((3,)),
             pltpu.SemaphoreType.DMA((groups,)),
@@ -190,18 +197,23 @@
     )(array)
 
 
-def regroup_body(*refs, half):
-    groups = len(refs) - 2
-    sources, out, ordered = refs[:groups], refs[groups], refs[groups + 1]
+def regroup_body(*refs, half, groups):
+    sources, out, ordered = refs[:-2], refs[-2], refs[-1]
     me = lax.axis_index("freq")
+    depth = 2 * half
+    size = CH_DEV * depth
     for s in range(groups):
-        ordered[partner(me, s, groups, -1)] = sources[s][...]
-    depth = 2 * half
+        if len(sources) == groups:
+            piece = sources[s][0:size]
+        else:
+            piece = sources[1][(s - 1) * size : s * size] if s else sources[0][...]
+        ordered[partner(me, s, groups, -1)] = piece
     lane = lax.broadcasted_iota(jnp.int32, (depth, LANES), 1)
     for pair in range(groups // 2):
         for k in range(CH_DEV):
-            left = ordered[2 * pair, k].astype(jnp.float32)
-            right = ordered[2 * pair + 1, k].astype(jnp.float32)
+            rows = slice(k * depth, (k + 1) * depth)
+            left = ordered[2 * pair, rows].astype(jnp.float32)
+            right = ordered[2 * pair + 1, rows].astype(jnp.float32)
             early = jnp.where(lane < LANES // 2, left, pltpu.roll(right, LANES // 2, 1))
             late = jnp.where(lane < LANES // 2, pltpu.roll(left, LANES // 2, 1), right)
             at = pl.ds(pair * LANES, LANES)
@@ -209,16 +221,34 @@
             out[k, depth : 2 * depth, at] = late.astype(jnp.bfloat16)
 
 
-def regroup(sources, half):
-    groups = len(sources)
+def regroup(sources, half, groups):
     shape = (CH_DEV, 4 * half, groups * LANES // 2)
     return pl.pallas_call(
-        functools.partial(regroup_body, half=half),
+        functools.partial(regroup_body, half=half, groups=groups),
         out_shape=jax.ShapeDtypeStruct(shape, jnp.bfloat16),
-        scratch_shapes=[pltpu.VMEM((groups,) + sources[0].shape, jnp.bfloat16)],
+        scratch_shapes=[pltpu.VMEM((groups, CH_DEV * 2 * half, LANES), jnp.bfloat16)],
         compiler_params=pltpu.CompilerParams(vmem_limit_bytes=4 * 2**20),
         name="regroup",
     )(*sources)
+
+
+def stack_body(*refs, count):
+    size = refs[-1].shape[0] // count
+    for index in range(count):
+        refs[-1][index * size : (index + 1) * size] = refs[index][0:size]
+
+
+def stack(pieces, after):
+    rows, lanes = pieces[0].shape
+    return pl.pallas_call(
+        functools.partial(stack_body, count=len(pieces)),
+        out_shape=jax.ShapeDtypeStruct((len(pieces) * (rows - PAD), lanes), jnp.bfloat16),
+        in_specs=[pl.BlockSpec(memory_space=pltpu.VMEM)] * len(pieces)
+        + [pl.BlockSpec(memory_space=pl.ANY)] * len(after),
+        out_specs=pl.BlockSpec(memory_space=pltpu.VMEM),
+        compiler_params=pltpu.CompilerParams(vmem_limit_bytes=2 * 2**20),
+        name="stack",
+    )(*pieces, *after)
 
 
 def products_body(*refs, half):
@@ -309,44 +339,31 @@
     return [sent[0]] + [lax.ppermute(sent[s], "freq", moves[s]) for s in range(1, groups)]
 
 
-def gather(mine):
+def to_columns(mine, core):
+    place = lambda x, y, c: x * 4 + y * 2 + c
+    pairs = [(place(x, y, core), place(1 - x, x, y)) for x in range(2) for y in range(2)]
+    return lax.ppermute(mine, ("row", "col"), pairs)
+
+
+def fast(samples, input_gains, filter_taps):
+    groups = lax.axis_size("freq")
+    half = SPEC // 2
     other_core = [(0, 1), (1, 0), (2, 3), (3, 2)]
     other_y = [(0, 2), (2, 0), (1, 3), (3, 1)]
-    place = lambda x, y, c: x * 4 + y * 2 + c
-    far_y = lax.ppermute(mine, "col", other_y)
-    columns = [
-        lax.ppermute(
-            mine,
-            ("row", "col"),
-            [(place(x, y, c), place(1 - x, x, y)) for x in range(2) for y in range(2)],
-        )
-        for c in range(2)
-    ]
+    sent = channelize(samples, input_gains, filter_taps, 0, half, CUTS, groups)
+    turned = exchange(sent, groups)
+    turned[1] = hold(turned[1])
+    across_own = lax.ppermute(turned[0], "col", other_y)
+    mine = regroup(turned, half, groups)
+    across_rest = lax.ppermute(stack(turned[1:], [across_own, mine]), "col", other_y)
+    columns = [to_columns(mine, core) for core in range(2)]
     near = lax.ppermute(mine, "col", other_core)
-    far = lax.ppermute(far_y, "col", other_core)
-    return [mine, near, far_y, far], columns
-
-
-def fast(samples, input_gains, filter_taps):
-    groups = lax.axis_size("freq")
-    parts = PARTS
-    half = SPEC // 2 // parts
-    row_blocks, col_blocks = [], []
-    for part in range(parts):
-        sent = channelize(
-            samples, input_gains, filter_taps, part * 2 * half, half, CUTS, groups
-        )
-        turned = exchange(sent, groups)
-        turned[1] = hold(turned[1])
-        mine = regroup(turned, half)
-        rows, columns = gather(mine)
-        row_blocks.append(rows)
-        col_blocks.append(columns)
-    return tuple(products(row_blocks, col_blocks, half))
-
-
-PARTS = 1
-CUTS = (0, 3, 7, 11, 15, 19, 23, 27, 31, 35)
+    across = regroup([across_own, across_rest], half, groups)
+    far = lax.ppermute(across, "col", other_core)
+    return tuple(products([(mine, near, across, far)], [columns], half))
+
+
+CUTS = (0, 3, 8, 13, 18, 23, 27, 31, 35)
 
 
 def dft_table(channels):

time: 42.3 us -> 42 us (level)
  the two profiles are of different devices: /device:TPU:11 before, /device:TPU:3 now
where the time goes in v5:
time: 42 us; the launch traced here: 41.9 us
  starting transfers between devices  18.1 us (43%)
  Pallas kernels  17.5 us (42%)
  waiting for transfers between devices  5.53 us (13%)
  between operations  0.7 us (2%)
    pallas_call x1, Pallas kernels, channelize(): pl.pallas_call(functools.partial(channelize_body, first=first, half=half,...  13.1 us
    ppermute x2, starting transfers between devices, to_columns(): return lax.ppermute(mine, ('row', 'col'), pairs)  6.92 us
    ppermute x3, starting transfers between devices, exchange(): lax.ppermute(sent[s], 'freq', moves[s])  5.64 us
    pallas_call x1, Pallas kernels, products(): pl.pallas_call(functools.partial(products_body, half=half), in_specs=[pl....  4.03 us
    ppermute x2, waiting for transfers between devices, to_columns(): return lax.ppermute(mine, ('row', 'col'), pairs)  3.38 us
    ppermute x1, starting transfers between devices, fast(): far = lax.ppermute(across, 'col', other_core)  3.27 us
    ppermute x3, waiting for transfers between devices, exchange(): lax.ppermute(sent[s], 'freq', moves[s])  2.14 us
    ppermute x1, starting transfers between devices, fast(): across_own = lax.ppermute(turned[0], 'col', other_y)  1.24 us
  transfers between devices with their start and end apart: 9, of which 3 were waited for; matrix products, arithmetic and copies ran while one was open for 0% of the time, Pallas kernels for 1%

profile of v5, /device:TPU:3, one launch (start us, length us, event | category | flops | bytes accessed | tf_op | source)
XLA Modules:
  0.0 41.9 jit_solution(10241065561450209700)
XLA Ops:
  0.6 13.1 %channelize.1 = (bf16[256,128]{1,0:T(8,128)(2,1)}, bf16[272,128]{1,0:T(8,128)(2,1)}, bf16[272,128]{1,0:T(8,128)(2,1)}, bf16[272,128]{1,0:T(8,128)(2,1)}) custom-call(f32[1,64]{1,0:T(1,128)} %bitcast.1, f32[4,1024]{1,0:T(4,128)} %taps_hbm.1, bf16[32,2048]{1,0:T(8,128)(2,1)} %constant.3.table_hbm, s32[2,64,68608]{2,1,0:T(8,128)} %samples_ref.1), custom_call_target="tpu_custom_call" | custom-call | flops 4496293888 | bytes 35127296 | tf_op jit(solution)/shard_map/channelize/pallas_call | solution.py:150
  13.7 2.4 %collective-permute-start = (bf16[272,128]{1,0:T(8,128)(2,1)}, bf16[272,128]{1,0:T(8,128)(2,1)S(1)}, u32[]{:S(2)}, u32[]{:S(2)}) collective-permute-start(bf16[272,128]{1,0:T(8,128)(2,1)} %get-tuple-element.7), channel_id=1, source_target_pairs={{0,16},{8,24},{16,0},{24,8},{1,17},{9,25},{17,1},{25,9},{2,18},{10... | collective-permute-start | bytes 208904 | tf_op jit(solution)/shard_map/ppermute | solution.py:339
  16.1 1.2 %collective-permute-start.4 = (bf16[256,128]{1,0:T(8,128)(2,1)}, bf16[256,128]{1,0:T(8,128)(2,1)S(1)}, u32[]{:S(2)}, u32[]{:S(2)}) collective-permute-start(bf16[256,128]{1,0:T(8,128)(2,1)} %get-tuple-element.6.refs_0_), channel_id=1, source_target_pairs={{0,2},{2,0},{1,3},{3,1},{4,6},{6,4},{5,7},{7,5},{8,10},{10,8},{9,1... | collective-permute-start | bytes 196616 | tf_op jit(solution)/shard_map/ppermute | solution.py:356
  17.4 1.3 %collective-permute-start.1 = (bf16[272,128]{1,0:T(8,128)(2,1)}, bf16[272,128]{1,0:T(8,128)(2,1)S(1)}, u32[]{:S(2)}, u32[]{:S(2)}) collective-permute-start(bf16[272,128]{1,0:T(8,128)(2,1)} %get-tuple-element.8), channel_id=1, source_target_pairs={{0,8},{8,16},{16,24},{24,0},{1,9},{9,17},{17,25},{25,1},{2,10},{10... | collective-permute-start | bytes 208904 | tf_op jit(solution)/shard_map/ppermute | solution.py:339
  18.7 0.0 copy-start
  18.7 2.0 %collective-permute-start.2 = (bf16[272,128]{1,0:T(8,128)(2,1)}, bf16[272,128]{1,0:T(8,128)(2,1)S(1)}, u32[]{:S(2)}, u32[]{:S(2)}) collective-permute-start(bf16[272,128]{1,0:T(8,128)(2,1)} %get-tuple-element.9), channel_id=1, source_target_pairs={{0,24},{8,0},{16,8},{24,16},{1,25},{9,1},{17,9},{25,17},{2,26},{10... | collective-permute-start | bytes 208904 | tf_op jit(solution)/shard_map/ppermute | solution.py:339
  20.6 0.0 collective-permute-done.source
  20.6 2.0 %collective-permute-done.1.refs_2_.refs_1_ = bf16[272,128]{1,0:T(8,128)(2,1)S(1)} collective-permute-done((bf16[272,128]{1,0:T(8,128)(2,1)}, bf16[272,128]{1,0:T(8,128)(2,1)S(1)}, u32[]{:S(2)}, u32[]{:S(2)}) %collective-permute-start.1) | collective-permute-done | bytes 69664 | tf_op jit(solution)/shard_map/ppermute | solution.py:339
  22.6 0.1 collective-permute-done.2.refs_3_.refs_2_
  22.8 0.0 copy-done
  22.8 0.2 regroup.2.refs_4_.refs_0_
  23.0 0.0 collective-permute-done.4.refs_3_.refs_0_
  23.0 0.6 %collective-permute-start.5 = (bf16[768,128]{1,0:T(8,128)(2,1)S(1)}, bf16[768,128]{1,0:T(8,128)(2,1)S(1)}, u32[]{:S(2)}, u32[]{:S(2)}) collective-permute-start(bf16[768,128]{1,0:T(8,128)(2,1)S(1)} %stack.1), channel_id=1, source_target_pairs={{0,2},{2,0},{1,3},{3,1},{4,6},{6,4},{5,7},{7,5},{8,10},{10,8},{9,1... | collective-permute-start | bytes 589832 | tf_op jit(solution)/shard_map/ppermute | solution.py:358
  23.6 5.6 %collective-permute-start.8 = (bf16[4,128,256]{2,1,0:T(8,128)(2,1)S(1)}, bf16[4,128,256]{2,1,0:T(8,128)(2,1)S(1)}, u32[]{:S(2)}, u32[]{:S(2)}) collective-permute-start(bf16[4,128,256]{2,1,0:T(8,128)(2,1)S(1)} %regroup.2.refs_4_.refs_0_), channel_id=1, source_target_pairs={{1,4},{3,5},{5,2},{7,3},{9,12},{11,13},{13,10},{15,11},{17,20},{19... | collective-permute-start | bytes 786440 | tf_op jit(solution)/shard_map/ppermute | solution.py:345
  29.2 1.3 %collective-permute-start.7 = (bf16[4,128,256]{2,1,0:T(8,128)(2,1)S(1)}, bf16[4,128,256]{2,1,0:T(8,128)(2,1)S(1)}, u32[]{:S(2)}, u32[]{:S(2)}) collective-permute-start(bf16[4,128,256]{2,1,0:T(8,128)(2,1)S(1)} %regroup.2.refs_4_.refs_0_), channel_id=1, source_target_pairs={{0,4},{2,5},{4,2},{6,3},{8,12},{10,13},{12,10},{14,11},{16,20},{18... | collective-permute-start | bytes 786440 | tf_op jit(solution)/shard_map/ppermute | solution.py:345
  30.5 0.5 %collective-permute-start.3 = (bf16[4,128,256]{2,1,0:T(8,128)(2,1)S(1)}, bf16[4,128,256]{2,1,0:T(8,128)(2,1)S(1)}, u32[]{:S(2)}, u32[]{:S(2)}) collective-permute-start(bf16[4,128,256]{2,1,0:T(8,128)(2,1)S(1)} %regroup.2.refs_4_.refs_0_), channel_id=1, source_target_pairs={{0,1},{1,0},{2,3},{3,2},{4,5},{5,4},{6,7},{7,6},{8,9},{9,8},{10,11... | collective-permute-start | bytes 786440 | tf_op jit(solution)/shard_map/ppermute | solution.py:360
  31.0 0.0 collective-permute-done.5.refs_1_
  31.0 0.2 regroup.3.refs_2_
  31.2 3.3 %collective-permute-start.6 = (bf16[4,128,256]{2,1,0:T(8,128)(2,1)S(1)}, bf16[4,128,256]{2,1,0:T(8,128)(2,1)S(1)}, u32[]{:S(2)}, u32[]{:S(2)}) collective-permute-start(bf16[4,128,256]{2,1,0:T(8,128)(2,1)S(1)} %regroup.3.refs_2_), channel_id=1, source_target_pairs={{0,1},{1,0},{2,3},{3,2},{4,5},{5,4},{6,7},{7,6},{8,9},{9,8},{10,11... | collective-permute-start | bytes 786440 | tf_op jit(solution)/shard_map/ppermute | solution.py:362
  34.4 0.0 collective-permute-done.8.refs_5_
  34.4 3.4 %collective-permute-done.7.refs_4_ = bf16[4,128,256]{2,1,0:T(8,128)(2,1)S(1)} collective-permute-done((bf16[4,128,256]{2,1,0:T(8,128)(2,1)S(1)}, bf16[4,128,256]{2,1,0:T(8,128)(2,1)S(1)}, u32[]{:S(2)}, u32[]{:S(2)}) %collective-permute-start.7) | collective-permute-done | bytes 262176 | tf_op jit(solution)/shard_map/ppermute | solution.py:345
  37.8 0.0 collective-permute-done.3.refs_1_
  37.8 0.0 collective-permute-done.6.refs_3_
  37.8 4.0 %products.1 = (bf16[4,1024,512]{2,1,0:T(8,128)(2,1)}, bf16[4,1024,512]{2,1,0:T(8,128)(2,1)}) custom-call(bf16[4,128,256]{2,1,0:T(8,128)(2,1)S(1)} %regroup.2.refs_4_.refs_0_, bf16[4,128,256]{2,1,0:T(8,128)(2,1)S(1)} %collective-permute-done.3.refs_1_, bf16[4,128,256]{2,1,0:T(8,128)(2,1)S(1)} %regroup.3.refs_2_, ...), custom_call_target="tpu_custom_call" | custom-call | flops 1073741824 | bytes 8388608 | tf_op jit(solution)/shard_map/products/pallas_call | solution.py:313
  (2 shorter events, 0.0 us)
Async XLA Ops:
  13.7 6.9 %collective-permute-start = (bf16[272,128]{1,0:T(8,128)(2,1)}, bf16[272,128]{1,0:T(8,128)(2,1)S(1)}, u32[]{:S(2)}, u32[]{:S(2)}) collective-permute-start(bf16[272,128]{1,0:T(8,128)(2,1)} %get-tuple-element.7), channel_id=1, source_target_pairs={{0,16},{8,24},{16,0},{24,8},{1,17},{9,25},{17,1},{25,9},{2,18},{10... | collective-permute-start | bytes 208904 | tf_op jit(solution)/shard_map/ppermute | solution.py:339
  16.1 6.8 %collective-permute-start.4 = (bf16[256,128]{1,0:T(8,128)(2,1)}, bf16[256,128]{1,0:T(8,128)(2,1)S(1)}, u32[]{:S(2)}, u32[]{:S(2)}) collective-permute-start(bf16[256,128]{1,0:T(8,128)(2,1)} %get-tuple-element.6.refs_0_), channel_id=1, source_target_pairs={{0,2},{2,0},{1,3},{3,1},{4,6},{6,4},{5,7},{7,5},{8,10},{10,8},{9,1... | collective-permute-start | bytes 196616 | tf_op jit(solution)/shard_map/ppermute | solution.py:356
  17.4 5.3 %collective-permute-start.1 = (bf16[272,128]{1,0:T(8,128)(2,1)}, bf16[272,128]{1,0:T(8,128)(2,1)S(1)}, u32[]{:S(2)}, u32[]{:S(2)}) collective-permute-start(bf16[272,128]{1,0:T(8,128)(2,1)} %get-tuple-element.8), channel_id=1, source_target_pairs={{0,8},{8,16},{16,24},{24,0},{1,9},{9,17},{17,25},{25,1},{2,10},{10... | collective-permute-start | bytes 208904 | tf_op jit(solution)/shard_map/ppermute | solution.py:339
  18.7 4.1 %copy-start = (bf16[256,128]{1,0:T(8,128)(2,1)S(1)}, bf16[256,128]{1,0:T(8,128)(2,1)}, u32[]{:S(2)}) copy-start(bf16[256,128]{1,0:T(8,128)(2,1)} %get-tuple-element.6.refs_0_) | copy-start | bytes 196612
  18.7 4.1 %collective-permute-start.2 = (bf16[272,128]{1,0:T(8,128)(2,1)}, bf16[272,128]{1,0:T(8,128)(2,1)S(1)}, u32[]{:S(2)}, u32[]{:S(2)}) collective-permute-start(bf16[272,128]{1,0:T(8,128)(2,1)} %get-tuple-element.9), channel_id=1, source_target_pairs={{0,24},{8,0},{16,8},{24,16},{1,25},{9,1},{17,9},{25,17},{2,26},{10... | collective-permute-start | bytes 208904 | tf_op jit(solution)/shard_map/ppermute | solution.py:339
  23.0 8.0 %collective-permute-start.5 = (bf16[768,128]{1,0:T(8,128)(2,1)S(1)}, bf16[768,128]{1,0:T(8,128)(2,1)S(1)}, u32[]{:S(2)}, u32[]{:S(2)}) collective-permute-start(bf16[768,128]{1,0:T(8,128)(2,1)S(1)} %stack.1), channel_id=1, source_target_pairs={{0,2},{2,0},{1,3},{3,1},{4,6},{6,4},{5,7},{7,5},{8,10},{10,8},{9,1... | collective-permute-start | bytes 589832 | tf_op jit(solution)/shard_map/ppermute | solution.py:358
  23.6 10.8 %collective-permute-start.8 = (bf16[4,128,256]{2,1,0:T(8,128)(2,1)S(1)}, bf16[4,128,256]{2,1,0:T(8,128)(2,1)S(1)}, u32[]{:S(2)}, u32[]{:S(2)}) collective-permute-start(bf16[4,128,256]{2,1,0:T(8,128)(2,1)S(1)} %regroup.2.refs_4_.refs_0_), channel_id=1, source_target_pairs={{1,4},{3,5},{5,2},{7,3},{9,12},{11,13},{13,10},{15,11},{17,20},{19... | collective-permute-start | bytes 786440 | tf_op jit(solution)/shard_map/ppermute | solution.py:345
  29.2 8.6 %collective-permute-start.7 = (bf16[4,128,256]{2,1,0:T(8,128)(2,1)S(1)}, bf16[4,128,256]{2,1,0:T(8,128)(2,1)S(1)}, u32[]{:S(2)}, u32[]{:S(2)}) collective-permute-start(bf16[4,128,256]{2,1,0:T(8,128)(2,1)S(1)} %regroup.2.refs_4_.refs_0_), channel_id=1, source_target_pairs={{0,4},{2,5},{4,2},{6,3},{8,12},{10,13},{12,10},{14,11},{16,20},{18... | collective-permute-start | bytes 786440 | tf_op jit(solution)/shard_map/ppermute | solution.py:345
  30.5 7.3 %collective-permute-start.3 = (bf16[4,128,256]{2,1,0:T(8,128)(2,1)S(1)}, bf16[4,128,256]{2,1,0:T(8,128)(2,1)S(1)}, u32[]{:S(2)}, u32[]{:S(2)}) collective-permute-start(bf16[4,128,256]{2,1,0:T(8,128)(2,1)S(1)} %regroup.2.refs_4_.refs_0_), channel_id=1, source_target_pairs={{0,1},{1,0},{2,3},{3,2},{4,5},{5,4},{6,7},{7,6},{8,9},{9,8},{10,11... | collective-permute-start | bytes 786440 | tf_op jit(solution)/shard_map/ppermute | solution.py:360
  31.2 6.7 %collective-permute-start.6 = (bf16[4,128,256]{2,1,0:T(8,128)(2,1)S(1)}, bf16[4,128,256]{2,1,0:T(8,128)(2,1)S(1)}, u32[]{:S(2)}, u32[]{:S(2)}) collective-permute-start(bf16[4,128,256]{2,1,0:T(8,128)(2,1)S(1)} %regroup.3.refs_2_), channel_id=1, source_target_pairs={{0,1},{1,0},{2,3},{3,2},{4,5},{5,4},{6,7},{7,6},{8,9},{9,8},{10,11... | collective-permute-start | bytes 786440 | tf_op jit(solution)/shard_map/ppermute | solution.py:362

commit v6 on v5

--- a/solution.py
+++ b/solution.py
@@ -19,7 +19,7 @@
 VMEM_BYTES = 60 * 2**20
 
 
-SHIFTS = (0, 2, 1, 3)
+SHIFTS = (0, 1, 2, 3)
 
 
 def partner(me, s, groups, sign=1):

time: 42 us -> 41.5 us (0.988)
  the two profiles are of different devices: /device:TPU:3 before, /device:TPU:11 now
where the time goes in v6:
time: 41.5 us; the launch traced here: 40.7 us
  Pallas kernels  17.5 us (42%)
  starting transfers between devices  12.7 us (31%)
  waiting for transfers between devices  9.82 us (24%)
  between operations  0.7 us (2%)
    pallas_call x1, Pallas kernels, channelize(): pl.pallas_call(functools.partial(channelize_body, first=first, half=half,...  13.1 us
    ppermute x2, waiting for transfers between devices, to_columns(): return lax.ppermute(mine, ('row', 'col'), pairs)  5.84 us
    ppermute x2, starting transfers between devices, to_columns(): return lax.ppermute(mine, ('row', 'col'), pairs)  4.63 us
    pallas_call x1, Pallas kernels, products(): pl.pallas_call(functools.partial(products_body, half=half), in_specs=[pl....  4.04 us
    ppermute x3, waiting for transfers between devices, exchange(): lax.ppermute(sent[s], 'freq', moves[s])  3.97 us
    ppermute x3, starting transfers between devices, exchange(): lax.ppermute(sent[s], 'freq', moves[s])  3.83 us
    ppermute x1, starting transfers between devices, fast(): lax.ppermute(stack(turned[1:], [across_own, mine]), 'col', other_y)  1.71 us
    ppermute x1, starting transfers between devices, fast(): across_own = lax.ppermute(turned[0], 'col', other_y)  1.24 us
  transfers between devices with their start and end apart: 9, of which 4 were waited for; matrix products, arithmetic and copies ran while one was open for 0% of the time, Pallas kernels for 1%

profile of v6, /device:TPU:11, one launch (start us, length us, event | category | flops | bytes accessed | tf_op | source)
XLA Modules:
  0.0 40.7 jit_solution(1722944769079733188)
XLA Ops:
  0.6 13.1 %channelize.1 = (bf16[256,128]{1,0:T(8,128)(2,1)}, bf16[272,128]{1,0:T(8,128)(2,1)}, bf16[272,128]{1,0:T(8,128)(2,1)}, bf16[272,128]{1,0:T(8,128)(2,1)}) custom-call(f32[1,64]{1,0:T(1,128)} %bitcast.1, f32[4,1024]{1,0:T(4,128)} %taps_hbm.1, bf16[32,2048]{1,0:T(8,128)(2,1)} %constant.3.table_hbm, s32[2,64,68608]{2,1,0:T(8,128)} %samples_ref.1), custom_call_target="tpu_custom_call" | custom-call | flops 4496293888 | bytes 35127296 | tf_op jit(solution)/shard_map/channelize/pallas_call | solution.py:150
  13.7 1.4 %collective-permute-start = (bf16[272,128]{1,0:T(8,128)(2,1)}, bf16[272,128]{1,0:T(8,128)(2,1)S(1)}, u32[]{:S(2)}, u32[]{:S(2)}) collective-permute-start(bf16[272,128]{1,0:T(8,128)(2,1)} %get-tuple-element.7), channel_id=1, source_target_pairs={{0,8},{8,16},{16,24},{24,0},{1,9},{9,17},{17,25},{25,1},{2,10},{10... | collective-permute-start | bytes 208904 | tf_op jit(solution)/shard_map/ppermute | solution.py:339
  15.1 1.2 %collective-permute-start.4 = (bf16[256,128]{1,0:T(8,128)(2,1)}, bf16[256,128]{1,0:T(8,128)(2,1)S(1)}, u32[]{:S(2)}, u32[]{:S(2)}) collective-permute-start(bf16[256,128]{1,0:T(8,128)(2,1)} %get-tuple-element.6.refs_0_), channel_id=1, source_target_pairs={{0,2},{2,0},{1,3},{3,1},{4,6},{6,4},{5,7},{7,5},{8,10},{10,8},{9,1... | collective-permute-start | bytes 196616 | tf_op jit(solution)/shard_map/ppermute | solution.py:356
  16.3 1.1 %collective-permute-start.1 = (bf16[272,128]{1,0:T(8,128)(2,1)}, bf16[272,128]{1,0:T(8,128)(2,1)S(1)}, u32[]{:S(2)}, u32[]{:S(2)}) collective-permute-start(bf16[272,128]{1,0:T(8,128)(2,1)} %get-tuple-element.8), channel_id=1, source_target_pairs={{0,16},{8,24},{16,0},{24,8},{1,17},{9,25},{17,1},{25,9},{2,18},{10... | collective-permute-start | bytes 208904 | tf_op jit(solution)/shard_map/ppermute | solution.py:339
  17.4 0.0 copy-start
  17.4 1.4 %collective-permute-start.2 = (bf16[272,128]{1,0:T(8,128)(2,1)}, bf16[272,128]{1,0:T(8,128)(2,1)S(1)}, u32[]{:S(2)}, u32[]{:S(2)}) collective-permute-start(bf16[272,128]{1,0:T(8,128)(2,1)} %get-tuple-element.9), channel_id=1, source_target_pairs={{0,24},{8,0},{16,8},{24,16},{1,25},{9,1},{17,9},{25,17},{2,26},{10... | collective-permute-start | bytes 208904 | tf_op jit(solution)/shard_map/ppermute | solution.py:339
  18.8 0.0 collective-permute-done.source
  18.8 1.8 %collective-permute-done.1.refs_2_.refs_1_ = bf16[272,128]{1,0:T(8,128)(2,1)S(1)} collective-permute-done((bf16[272,128]{1,0:T(8,128)(2,1)}, bf16[272,128]{1,0:T(8,128)(2,1)S(1)}, u32[]{:S(2)}, u32[]{:S(2)}) %collective-permute-start.1) | collective-permute-done | bytes 69664 | tf_op jit(solution)/shard_map/ppermute | solution.py:339
  20.7 2.1 %collective-permute-done.2.refs_3_.refs_2_ = bf16[272,128]{1,0:T(8,128)(2,1)S(1)} collective-permute-done((bf16[272,128]{1,0:T(8,128)(2,1)}, bf16[272,128]{1,0:T(8,128)(2,1)S(1)}, u32[]{:S(2)}, u32[]{:S(2)}) %collective-permute-start.2) | collective-permute-done | bytes 69664 | tf_op jit(solution)/shard_map/ppermute | solution.py:339
  22.8 0.0 copy-done
  22.8 0.2 regroup.2.refs_4_.refs_0_
  23.0 0.0 collective-permute-done.4.refs_3_.refs_0_
  23.0 1.7 %collective-permute-start.5 = (bf16[768,128]{1,0:T(8,128)(2,1)S(1)}, bf16[768,128]{1,0:T(8,128)(2,1)S(1)}, u32[]{:S(2)}, u32[]{:S(2)}) collective-permute-start(bf16[768,128]{1,0:T(8,128)(2,1)S(1)} %stack.1), channel_id=1, source_target_pairs={{0,2},{2,0},{1,3},{3,1},{4,6},{6,4},{5,7},{7,5},{8,10},{10,8},{9,1... | collective-permute-start | bytes 589832 | tf_op jit(solution)/shard_map/ppermute | solution.py:358
  24.7 3.3 %collective-permute-start.8 = (bf16[4,128,256]{2,1,0:T(8,128)(2,1)S(1)}, bf16[4,128,256]{2,1,0:T(8,128)(2,1)S(1)}, u32[]{:S(2)}, u32[]{:S(2)}) collective-permute-start(bf16[4,128,256]{2,1,0:T(8,128)(2,1)S(1)} %regroup.2.refs_4_.refs_0_), channel_id=1, source_target_pairs={{1,4},{3,5},{5,2},{7,3},{9,12},{11,13},{13,10},{15,11},{17,20},{19... | collective-permute-start | bytes 786440 | tf_op jit(solution)/shard_map/ppermute | solution.py:345
  28.1 1.3 %collective-permute-start.7 = (bf16[4,128,256]{2,1,0:T(8,128)(2,1)S(1)}, bf16[4,128,256]{2,1,0:T(8,128)(2,1)S(1)}, u32[]{:S(2)}, u32[]{:S(2)}) collective-permute-start(bf16[4,128,256]{2,1,0:T(8,128)(2,1)S(1)} %regroup.2.refs_4_.refs_0_), channel_id=1, source_target_pairs={{0,4},{2,5},{4,2},{6,3},{8,12},{10,13},{12,10},{14,11},{16,20},{18... | collective-permute-start | bytes 786440 | tf_op jit(solution)/shard_map/ppermute | solution.py:345
  29.4 0.5 %collective-permute-start.3 = (bf16[4,128,256]{2,1,0:T(8,128)(2,1)S(1)}, bf16[4,128,256]{2,1,0:T(8,128)(2,1)S(1)}, u32[]{:S(2)}, u32[]{:S(2)}) collective-permute-start(bf16[4,128,256]{2,1,0:T(8,128)(2,1)S(1)} %regroup.2.refs_4_.refs_0_), channel_id=1, source_target_pairs={{0,1},{1,0},{2,3},{3,2},{4,5},{5,4},{6,7},{7,6},{8,9},{9,8},{10,11... | collective-permute-start | bytes 786440 | tf_op jit(solution)/shard_map/ppermute | solution.py:360
  29.8 0.0 collective-permute-done.5.refs_1_
  29.8 0.2 regroup.3.refs_2_
  30.0 0.8 %collective-permute-start.6 = (bf16[4,128,256]{2,1,0:T(8,128)(2,1)S(1)}, bf16[4,128,256]{2,1,0:T(8,128)(2,1)S(1)}, u32[]{:S(2)}, u32[]{:S(2)}) collective-permute-start(bf16[4,128,256]{2,1,0:T(8,128)(2,1)S(1)} %regroup.3.refs_2_), channel_id=1, source_target_pairs={{0,1},{1,0},{2,3},{3,2},{4,5},{5,4},{6,7},{7,6},{8,9},{9,8},{10,11... | collective-permute-start | bytes 786440 | tf_op jit(solution)/shard_map/ppermute | solution.py:362
  30.8 1.9 %collective-permute-done.8.refs_5_ = bf16[4,128,256]{2,1,0:T(8,128)(2,1)S(1)} collective-permute-done((bf16[4,128,256]{2,1,0:T(8,128)(2,1)S(1)}, bf16[4,128,256]{2,1,0:T(8,128)(2,1)S(1)}, u32[]{:S(2)}, u32[]{:S(2)}) %collective-permute-start.8) | collective-permute-done | bytes 262176 | tf_op jit(solution)/shard_map/ppermute | solution.py:345
  32.7 3.9 %collective-permute-done.7.refs_4_ = bf16[4,128,256]{2,1,0:T(8,128)(2,1)S(1)} collective-permute-done((bf16[4,128,256]{2,1,0:T(8,128)(2,1)S(1)}, bf16[4,128,256]{2,1,0:T(8,128)(2,1)S(1)}, u32[]{:S(2)}, u32[]{:S(2)}) %collective-permute-start.7) | collective-permute-done | bytes 262176 | tf_op jit(solution)/shard_map/ppermute | solution.py:345
  36.7 0.0 collective-permute-done.3.refs_1_
  36.7 0.0 collective-permute-done.6.refs_3_
  36.7 4.0 %products.1 = (bf16[4,1024,512]{2,1,0:T(8,128)(2,1)}, bf16[4,1024,512]{2,1,0:T(8,128)(2,1)}) custom-call(bf16[4,128,256]{2,1,0:T(8,128)(2,1)S(1)} %regroup.2.refs_4_.refs_0_, bf16[4,128,256]{2,1,0:T(8,128)(2,1)S(1)} %collective-permute-done.3.refs_1_, bf16[4,128,256]{2,1,0:T(8,128)(2,1)S(1)} %regroup.3.refs_2_, ...), custom_call_target="tpu_custom_call" | custom-call | flops 1073741824 | bytes 8388608 | tf_op jit(solution)/shard_map/products/pallas_call | solution.py:313
  (2 shorter events, 0.0 us)
Async XLA Ops:
  13.7 5.1 %collective-permute-start = (bf16[272,128]{1,0:T(8,128)(2,1)}, bf16[272,128]{1,0:T(8,128)(2,1)S(1)}, u32[]{:S(2)}, u32[]{:S(2)}) collective-permute-start(bf16[272,128]{1,0:T(8,128)(2,1)} %get-tuple-element.7), channel_id=1, source_target_pairs={{0,8},{8,16},{16,24},{24,0},{1,9},{9,17},{17,25},{25,1},{2,10},{10... | collective-permute-start | bytes 208904 | tf_op jit(solution)/shard_map/ppermute | solution.py:339
  15.1 7.9 %collective-permute-start.4 = (bf16[256,128]{1,0:T(8,128)(2,1)}, bf16[256,128]{1,0:T(8,128)(2,1)S(1)}, u32[]{:S(2)}, u32[]{:S(2)}) collective-permute-start(bf16[256,128]{1,0:T(8,128)(2,1)} %get-tuple-element.6.refs_0_), channel_id=1, source_target_pairs={{0,2},{2,0},{1,3},{3,1},{4,6},{6,4},{5,7},{7,5},{8,10},{10,8},{9,1... | collective-permute-start | bytes 196616 | tf_op jit(solution)/shard_map/ppermute | solution.py:356
  16.3 4.3 %collective-permute-start.1 = (bf16[272,128]{1,0:T(8,128)(2,1)}, bf16[272,128]{1,0:T(8,128)(2,1)S(1)}, u32[]{:S(2)}, u32[]{:S(2)}) collective-permute-start(bf16[272,128]{1,0:T(8,128)(2,1)} %get-tuple-element.8), channel_id=1, source_target_pairs={{0,16},{8,24},{16,0},{24,8},{1,17},{9,25},{17,1},{25,9},{2,18},{10... | collective-permute-start | bytes 208904 | tf_op jit(solution)/shard_map/ppermute | solution.py:339
  17.4 5.4 %copy-start = (bf16[256,128]{1,0:T(8,128)(2,1)S(1)}, bf16[256,128]{1,0:T(8,128)(2,1)}, u32[]{:S(2)}) copy-start(bf16[256,128]{1,0:T(8,128)(2,1)} %get-tuple-element.6.refs_0_) | copy-start | bytes 196612
  17.4 5.4 %collective-permute-start.2 = (bf16[272,128]{1,0:T(8,128)(2,1)}, bf16[272,128]{1,0:T(8,128)(2,1)S(1)}, u32[]{:S(2)}, u32[]{:S(2)}) collective-permute-start(bf16[272,128]{1,0:T(8,128)(2,1)} %get-tuple-element.9), channel_id=1, source_target_pairs={{0,24},{8,0},{16,8},{24,16},{1,25},{9,1},{17,9},{25,17},{2,26},{10... | collective-permute-start | bytes 208904 | tf_op jit(solution)/shard_map/ppermute | solution.py:339
  23.0 6.8 %collective-permute-start.5 = (bf16[768,128]{1,0:T(8,128)(2,1)S(1)}, bf16[768,128]{1,0:T(8,128)(2,1)S(1)}, u32[]{:S(2)}, u32[]{:S(2)}) collective-permute-start(bf16[768,128]{1,0:T(8,128)(2,1)S(1)} %stack.1), channel_id=1, source_target_pairs={{0,2},{2,0},{1,3},{3,1},{4,6},{6,4},{5,7},{7,5},{8,10},{10,8},{9,1... | collective-permute-start | bytes 589832 | tf_op jit(solution)/shard_map/ppermute | solution.py:358
  24.7 8.0 %collective-permute-start.8 = (bf16[4,128,256]{2,1,0:T(8,128)(2,1)S(1)}, bf16[4,128,256]{2,1,0:T(8,128)(2,1)S(1)}, u32[]{:S(2)}, u32[]{:S(2)}) collective-permute-start(bf16[4,128,256]{2,1,0:T(8,128)(2,1)S(1)} %regroup.2.refs_4_.refs_0_), channel_id=1, source_target_pairs={{1,4},{3,5},{5,2},{7,3},{9,12},{11,13},{13,10},{15,11},{17,20},{19... | collective-permute-start | bytes 786440 | tf_op jit(solution)/shard_map/ppermute | solution.py:345
  28.1 8.6 %collective-permute-start.7 = (bf16[4,128,256]{2,1,0:T(8,128)(2,1)S(1)}, bf16[4,128,256]{2,1,0:T(8,128)(2,1)S(1)}, u32[]{:S(2)}, u32[]{:S(2)}) collective-permute-start(bf16[4,128,256]{2,1,0:T(8,128)(2,1)S(1)} %regroup.2.refs_4_.refs_0_), channel_id=1, source_target_pairs={{0,4},{2,5},{4,2},{6,3},{8,12},{10,13},{12,10},{14,11},{16,20},{18... | collective-permute-start | bytes 786440 | tf_op jit(solution)/shard_map/ppermute | solution.py:345
  29.4 7.3 %collective-permute-start.3 = (bf16[4,128,256]{2,1,0:T(8,128)(2,1)S(1)}, bf16[4,128,256]{2,1,0:T(8,128)(2,1)S(1)}, u32[]{:S(2)}, u32[]{:S(2)}) collective-permute-start(bf16[4,128,256]{2,1,0:T(8,128)(2,1)S(1)} %regroup.2.refs_4_.refs_0_), channel_id=1, source_target_pairs={{0,1},{1,0},{2,3},{3,2},{4,5},{5,4},{6,7},{7,6},{8,9},{9,8},{10,11... | collective-permute-start | bytes 786440 | tf_op jit(solution)/shard_map/ppermute | solution.py:360
  30.0 6.7 %collective-permute-start.6 = (bf16[4,128,256]{2,1,0:T(8,128)(2,1)S(1)}, bf16[4,128,256]{2,1,0:T(8,128)(2,1)S(1)}, u32[]{:S(2)}, u32[]{:S(2)}) collective-permute-start(bf16[4,128,256]{2,1,0:T(8,128)(2,1)S(1)} %regroup.3.refs_2_), channel_id=1, source_target_pairs={{0,1},{1,0},{2,3},{3,2},{4,5},{5,4},{6,7},{7,6},{8,9},{9,8},{10,11... | collective-permute-start | bytes 786440 | tf_op jit(solution)/shard_map/ppermute | solution.py:362
